TPU v7x, 256 devices: a whole 4x4x8 slice. The times are simulated.
256 devices in a mesh: rep: 8 (over x, core), shard: 32 (over y, z).
Axes of the slice: x: 4, y: 4, z: 8, core: 2. Of those that a mesh axis runs over, the one named last changes fastest.
Arguments:
- grads: bfloat16 [8, 5120, 1536], P('rep', 'shard'), may hold values from -2.5 to 2.5
- left_prev: float32 [64, 512, 512], P('shard'), as said below
- right_prev: float32 [64, 512, 512], P('shard'), as said below
- block_owner: int32 [30], replicated, may hold values from 0 to 31, as said below
- block_row: int32 [30], replicated, may hold values from 0 to 4608, as said below
- block_col: int32 [30], replicated, may hold values from 0 to 1024, as said below
Outputs:
- direction: bfloat16 [5120, 1536], P('shard')
- left_new: float32 [64, 512, 512], P('shard')
- right_new: float32 [64, 512, 512], P('shard')
Inputs may be any that keep to these rules, and one draw needn't show every extreme that they name: `block_owner`: each owner holds at most 2 blocks and some owner holds exactly 2. `block_row`: multiples of 512; together with block_col the blocks cover the 5120 x 1536 matrix, each entry once. `block_col`: multiples of 512. `left_prev`: each slot holds a symmetric positive definite matrix. `right_prev`: each slot holds a symmetric positive definite matrix.
All inputs are finite; a program needn't handle non-finite values.
Results may differ from a plain program's by a relative error of at most 0.022.
Values may be sent and summed in bfloat16 or wider, within the bound.
A program may use at most 128 MiB of HBM per device.

v0:
```python
import jax
import jax.numpy as jnp
from jax import lax
from jax.sharding import PartitionSpec as P

ITERS = 2


def slot_table(owner, per_owner):
    count = owner.shape[0]
    index = jnp.arange(count, dtype=jnp.int32)
    same = (owner[:, None] == owner[None, :]) & (index[None, :] < index[:, None])
    return owner * per_owner + jnp.sum(same.astype(jnp.int32), axis=1)


def inverse_root(mats, iterations):
    size = mats.shape[-1]
    highest = lax.Precision.HIGHEST
    ident = jnp.eye(size, dtype=jnp.float32)
    scale = jnp.trace(mats, axis1=1, axis2=2) / size
    coupled = mats / scale[:, None, None]
    factor = scale ** (-0.25)
    root = ident[None]
    for step in range(iterations):
        middle = (5.0 * ident - coupled) * 0.25
        if step == 0:
            root = factor[:, None, None] * middle
        else:
            root = jnp.einsum("kij,kjl->kil", root, middle, precision=highest)
        if step + 1 < iterations:
            square = jnp.einsum("kij,kjl->kil", middle, middle, precision=highest)
            fourth = jnp.einsum("kij,kjl->kil", square, square, precision=highest)
            coupled = jnp.einsum("kij,kjl->kil", fourth, coupled, precision=highest)
    return root


def place_rows(returned, col_grid, block, col_blocks):
    placing = (
        (col_grid // block)[:, :, None] == jnp.arange(col_blocks, dtype=jnp.int32)[None, None, :]
    ).astype(jnp.bfloat16)
    placed = jnp.einsum("soc,sork->rck", placing, returned, preferred_element_type=jnp.float32)
    return placed.reshape(returned.shape[2], col_blocks * block).astype(jnp.bfloat16)


def body(grads, left_prev, right_prev, block_owner, block_row, block_col):
    highest = lax.Precision.HIGHEST
    shards = lax.axis_size("shard")
    myself = lax.axis_index("shard")
    rows_dev = grads.shape[1]
    width_all = grads.shape[2]
    per_owner = left_prev.shape[0]
    block = left_prev.shape[1]
    col_blocks = width_all // block
    rows_all = shards * rows_dev
    row_blocks = rows_all // block
    total = lax.psum(grads[0].astype(jnp.float32).astype(jnp.bfloat16), "rep")
    slot_all = slot_table(block_owner, per_owner)
    every_slot = jnp.arange(shards * per_owner, dtype=jnp.int32)
    hit_all = (slot_all[None, :] == every_slot[:, None]).astype(jnp.int32)
    col_grid = jnp.sum(hit_all * block_col[None, :], axis=1).reshape(shards, per_owner).T
    wanted = myself * per_owner + jnp.arange(per_owner, dtype=jnp.int32)
    hit_mine = (slot_all[None, :] == wanted[:, None]).astype(jnp.int32)
    live = jnp.sum(hit_mine, axis=1)
    my_row = jnp.sum(hit_mine * block_row[None, :], axis=1)
    my_col = jnp.sum(hit_mine * block_col[None, :], axis=1)
    row_pick = (my_row // block)[:, None] == jnp.arange(row_blocks, dtype=jnp.int32)[None, :]
    col_pick = (
        (my_col // block)[:, None] == jnp.arange(col_blocks, dtype=jnp.int32)[None, :]
    ).astype(jnp.bfloat16)
    piece = lax.all_gather(total, "shard", axis=0, tiled=True)
    count = piece.shape[0]
    piece3 = piece.reshape(count, col_blocks, block)
    columns = jnp.einsum("sc,rck->srk", col_pick, piece3, preferred_element_type=jnp.float32)
    slab4 = columns.reshape(per_owner, row_blocks, block, block)
    blocks = jnp.einsum("sq,sqik->sik", row_pick.astype(jnp.float32), slab4, precision=highest)
    live_f = live.astype(jnp.float32)[:, None, None]
    blocks = blocks * live_f
    left_new = (left_prev + jnp.einsum("sik,sjk->sij", blocks, blocks, precision=highest)) * live_f
    right_new = (
        right_prev + jnp.einsum("ski,skj->sij", blocks, blocks, precision=highest)
    ) * live_f
    ident = jnp.eye(block, dtype=jnp.float32)
    stacked = jnp.concatenate([left_new, right_new], axis=0)
    live_both = jnp.concatenate([live, live], axis=0)[:, None, None] > 0
    roots = inverse_root(jnp.where(live_both, stacked, ident[None]), ITERS)
    precond = jnp.einsum("sik,skl->sil", roots[:per_owner], blocks, precision=highest)
    precond = jnp.einsum("sil,slj->sij", precond, roots[per_owner:], precision=highest)
    ratio = jnp.sqrt(
        jnp.sum(blocks * blocks, axis=(1, 2)) / (jnp.sum(precond * precond, axis=(1, 2)) + 1e-06)
    )
    dir_blocks = (precond * ratio[:, None, None]).astype(jnp.bfloat16)
    spread = row_pick.astype(jnp.bfloat16)[:, :, None, None] * dir_blocks[:, None, :, :]
    spread = spread.reshape(per_owner, shards, rows_dev, block)
    returned = lax.all_to_all(spread, "shard", split_axis=1, concat_axis=1, tiled=True)
    direction = place_rows(returned, col_grid, block, col_blocks)
    return (direction, left_new, right_new)


def solution(mesh):
    in_specs = (
        P("rep", "shard", None),
        P("shard", None, None),
        P("shard", None, None),
        P(),
        P(),
        P(),
    )
    out_specs = (P("shard", None), P("shard", None, None), P("shard", None, None))
    return jax.shard_map(body, mesh=mesh, in_specs=in_specs, out_specs=out_specs, check_vma=False)
```

profile of v0, /device:TPU:1, one launch (start us, length us, event | category | flops | bytes accessed | tf_op | source)
XLA Modules:
  0.0 681.9 jit_solution(17412951545436555565)
XLA Ops:
  7.9 69.8 %all-reduce.2.cloned.1.call-done = bf16[160,1536]{1,0:T(8,128)(2,1)} async-done(((bf16[160,1536]{1,0:T(8,128)(2,1)}), bf16[160,1536]{1,0:T(8,128)(2,1)}) %all-reduce.2.cloned.1.call-update) | async-done | bytes 491536 | tf_op jit(solution)/shard_map/psum | solution.py:56
  77.8 0.9 convert_reduce_fusion
  80.6 1.1 fusion.33
  81.9 134.8 %all-gather.2.cloned.1.call-done = bf16[5120,1536]{1,0:T(8,128)(2,1)} async-done(((bf16[160,1536]{1,0:T(8,128)(2,1)}), bf16[5120,1536]{1,0:T(8,128)(2,1)}) %all-gather.2.cloned.1.call-update) | async-done | bytes 15728656 | tf_op jit(solution)/shard_map/all_gather | solution.py:70
  216.7 20.7 %copy.30 = bf16[5120,1536]{0,1:T(8,128)(2,1)} copy(bf16[5120,1536]{1,0:T(8,128)(2,1)} %all-gather.2.cloned.1.call-done) | data formatting | bytes 31457280 | tf_op jit(solution)/shard_map/all_gather | solution.py:70
  237.4 20.7 %copy.31 = bf16[5120,512,3]{1,0,2:T(8,128)(2,1)} copy(bf16[5120,512,3]{0,1,2:T(8,128)(2,1)} %bitcast.53) | data formatting | bytes 31457280 | tf_op jit(solution)/shard_map/sc,rck->srk/dot_general | solution.py:73
  258.1 48.2 %fusion.2 = f32[2,10,512,512]{3,0,2,1:T(2,128)} fusion(bf16[10,512,512,3]{2,1,0,3:T(8,128)(2,1)} %bitcast.52, s32[2]{0:T(128)S(1)} %get-tuple-element.12), kind=kOutput, calls=%fused_computation.2 | convolution fusion | flops 31457286 | bytes 36700168 | tf_op jit(solution)/shard_map/sc,rck->srk/dot_general | solution.py:73
  306.3 22.6 %fusion = f32[2,1,512,512]{3,1,2,0:T(1,128)S(1)} fusion(f32[2,10,512,512]{3,0,2,1:T(2,128)} %fusion.2, pred[2,10,1,1]{1,0,2,3:T(4,128)(4,1)S(1)} %get-tuple-element.7), kind=kOutput, calls=%fused_computation | convolution fusion | flops 62914560 | bytes 23068692 | tf_op jit(solution)/shard_map/sq,sqik->sik/dot_general | solution.py:75
  329.5 4.2 add_multiply_fusion
  333.7 3.8 add_multiply_fusion.1
  337.6 1.4 select_reduce_fusion
  339.6 8.8 %fusion.9 = f32[4,512,512]{2,1,0:T(8,128)S(1)} fusion(f32[512,512]{1,0:T(8,128)S(1)} %copy-done.4, f32[2,512,512]{2,1,0:T(8,128)S(1)} %add_multiply_fusion, f32[2,512,512]{2,1,0:T(8,128)S(1)} %add_multiply_fusion.1, f32[4]{0:T(128)S(1)} %get-tuple-element.9, f32[512,512]{1,0:T(8,128)S(1)} %get-tuple-element.15, pred[4]{0:T(512)(128)(4,1)S(1)} %add_compare_fusion), kind=kOutput, calls=%fused_computation.11 | convolution fusion | flops 6447693824 | bytes 10485780 | tf_op jit(solution)/shard_map/kij,kjl->kil/dot_general | solution.py:31
  348.4 7.4 %fusion.58 = f32[4,512,512]{2,1,0:T(8,128)S(1)} fusion(f32[4,512,512]{2,1,0:T(8,128)S(1)} %fusion.9), kind=kOutput, calls=%fused_computation.89 | convolution fusion | flops 6442450944 | bytes 8388608 | tf_op jit(solution)/shard_map/kij,kjl->kil/dot_general | solution.py:32
  355.8 8.1 %fusion.55 = f32[4,512,512]{2,1,0:T(8,128)S(1)} fusion(f32[4,512,512]{2,1,0:T(8,128)S(1)} %fusion.58, f32[2,512,512]{2,1,0:T(8,128)S(1)} %add_multiply_fusion, f32[2,512,512]{2,1,0:T(8,128)S(1)} %add_multiply_fusion.1, f32[4]{0:T(128)S(1)} %get-tuple-element.9, f32[512,512]{1,0:T(8,128)S(1)} %get-tuple-element.15, pred[4]{0:T(512)(128)(4,1)S(1)} %add_compare_fusion), kind=kOutput, calls=%fused_computation.88 | convolution fusion | flops 6445596672 | bytes 13631508 | tf_op jit(solution)/shard_map/kij,kjl->kil/dot_general | solution.py:33
  363.9 8.5 %fusion.6 = f32[4,512,512]{2,1,0:T(8,128)S(1)} fusion(f32[4,512,512]{2,1,0:T(8,128)S(1)} %fusion.55, f32[4]{0:T(128)S(1)} %get-tuple-element.8, f32[512,512]{1,0:T(8,128)S(1)} %copy-done.4, f32[2,512,512]{2,1,0:T(8,128)S(1)} %add_multiply_fusion, f32[2,512,512]{2,1,0:T(8,128)S(1)} %add_multiply_fusion.1, f32[4]{0:T(128)S(1)} %get-tuple-element.9, ...), kind=kOutput, calls=%fused_computation.8 | convolution fusion | flops 6449790976 | bytes 14680100 | tf_op jit(solution)/shard_map/kij,kjl->kil/dot_general | solution.py:29
  372.4 3.9 fusion.25
  376.4 3.8 multiply_reduce_fusion
  380.5 5.1 mul.132
  385.6 6.0 broadcast_multiply_fusion
  391.6 30.5 %copy.34 = bf16[2,32,160,512]{3,0,2,1:T(2,128)(2,1)} copy(bf16[2,32,160,512]{3,2,1,0:T(8,128)(2,1)S(1)} %broadcast_multiply_fusion) | data formatting | bytes 20971520 | tf_op jit(solution)/shard_map/mul | solution.py:92
  422.1 5.7 all-to-all-start
  428.2 236.0 %all-to-all-done = bf16[2,32,160,512]{3,0,2,1:T(2,128)(2,1)} async-done(((bf16[2,32,160,512]{3,0,2,1:T(2,128)(2,1)}), bf16[2,32,160,512]{3,0,2,1:T(2,128)(2,1)}, u32[]{:S(2)}, u32[]{:S(2)}) %all-to-all-start) | async-done | bytes 10485792 | tf_op jit(solution)/shard_map/all_to_all | solution.py:94
  664.2 9.7 %fusion.26 = bf16[160,512,3]{1,2,0:T(4,128)(2,1)S(1)} fusion(bf16[2,32,160,512]{3,0,2,1:T(2,128)(2,1)} %all-to-all-done, s32[2,32]{1,0:T(2,128)S(1)} %copy.35), kind=kOutput, calls=%fused_computation.33 | convolution fusion | flops 31703232 | bytes 10977536 | tf_op jit(solution)/shard_map/soc,sork->rck/dot_general | solution.py:41
  673.9 0.9 copy.43
  (34 shorter events, 4.7 us)
Async XLA Ops:
  7.2 70.6 %all-reduce.2.cloned.1.call-start = ((), (), s32[]{:S(2)}) async-start(), calls=%async_computation.1 | async-start | bytes 983040 | tf_op jit(solution)/shard_map/psum | solution.py:56
  7.9 208.8 %all-gather.2.cloned.1.call-start = ((), (), s32[]{:S(2)}) async-start(), calls=%async_computation.2 | async-start | bytes 16220160 | tf_op jit(solution)/shard_map/all_gather | solution.py:70
  306.3 23.2 %copy-start.2 = (f32[2,512,512]{2,1,0:T(8,128)S(1)}, f32[2,512,512]{2,1,0:T(8,128)}, u32[]{:S(2)}) copy-start(f32[2,512,512]{2,1,0:T(8,128)} %param.8) | copy-start | bytes 6291460
  328.9 4.8 copy-start.3
  333.7 30.1 %copy-start = (f32[2,512,512]{2,1,0:T(8,128)}, f32[2,512,512]{2,1,0:T(8,128)S(1)}, u32[]{:S(2)}) copy-start(f32[2,512,512]{2,1,0:T(8,128)S(1)} %add_multiply_fusion) | copy-start | bytes 6291460
  337.6 26.3 %copy-start.1 = (f32[2,512,512]{2,1,0:T(8,128)}, f32[2,512,512]{2,1,0:T(8,128)S(1)}, u32[]{:S(2)}) copy-start(f32[2,512,512]{2,1,0:T(8,128)S(1)} %add_multiply_fusion.1) | copy-start | bytes 6291460
  337.6 2.0 copy-start.4
  422.1 5.7 copy-start.5
  422.1 242.1 %all-to-all-start = ((bf16[2,32,160,512]{3,0,2,1:T(2,128)(2,1)}), bf16[2,32,160,512]{3,0,2,1:T(2,128)(2,1)}, u32[]{:S(2)}, u32[]{:S(2)}) async-start(bf16[2,32,160,512]{3,0,2,1:T(2,128)(2,1)} %copy.34), calls=%async_computation | async-start | bytes 20971520 | tf_op jit(solution)/shard_map/all_to_all | solution.py:94
Sparse Core Ops, SparseCore 0:
  10.3 67.3 all-reduce.1
  80.7 136.0 all-gather.1
where the time goes:
time: 695 us; the launch traced here: 682 us
  waiting for transfers between devices  441 us (63%)
  matrix products  129 us (19%)
  local copies, waits for them, and re-layouts  78.9 us (11%)
  between operations  14.4 us (2%)
  other arithmetic  12.4 us (2%)
    all_to_all x1, waiting for transfers between devices, body(): lax.all_to_all(spread, 'shard', split_axis=1, concat_axis=1, tiled=True)  236 us
    all_gather x1, waiting for transfers between devices, body(): piece = lax.all_gather(total, 'shard', axis=0, tiled=True)  135 us
    psum x1, waiting for transfers between devices, body(): total = lax.psum(grads[0].astype(jnp.float32).astype(jnp.bfloat16), 'rep')  69.8 us
    dot_general x1, matrix products, body(): jnp.einsum('sc,rck->srk', col_pick, piece3, preferred_element_type=jnp.fl...  48.2 us
    mul x4, local copies, waits for them, and re-layouts, body(): row_pick.astype(jnp.bfloat16)[:, :, None, None] * dir_blocks[:, None, :, :]  35.8 us
    dot_general x1, matrix products, body(): jnp.einsum('sq,sqik->sik', row_pick.astype(jnp.float32), slab4, precision...  22.6 us
    dot_general x1, local copies, waits for them, and re-layouts, body(): jnp.einsum('sc,rck->srk', col_pick, piece3, preferred_element_type=jnp.fl...  20.7 us
    all_gather x1, local copies, waits for them, and re-layouts, body(): piece = lax.all_gather(total, 'shard', axis=0, tiled=True)  20.7 us
  transfers between devices with their start and end apart: 3, of which 3 were waited for; matrix products, arithmetic and copies ran while one was open for 1% of the time, Pallas kernels for 0%

commit v1 on v0

v1 whole, which is shorter than its diff:
```python
import jax
import jax.numpy as jnp
from jax import lax
from jax.experimental import pallas as pl
from jax.experimental.pallas import tpu as pltpu
from jax.sharding import PartitionSpec as P

BLK = 512
COLB = 3
ROWB = 10
CELLS = 30
SHARDS = 32
HALF = 16
TILES = 5
LANE = 128
SUB = 16
XS = 4
MESH = pl.DeviceIdType.MESH
BF = jnp.bfloat16
F32 = jnp.float32


def place():
    rep = lax.axis_index("rep")
    shard = lax.axis_index("shard")
    x = rep // 2
    h = rep % 2
    return rep, shard, x, h


def send(src, dst, send_sem, recv_sem, rep, shard):
    return pltpu.make_async_remote_copy(
        src_ref=src,
        dst_ref=dst,
        send_sem=send_sem,
        recv_sem=recv_sem,
        device_id=(rep, shard),
        device_id_type=MESH,
    )


def greet(barrier, rep, shard):
    pl.semaphore_signal(barrier, inc=1, device_id=(rep, shard), device_id_type=MESH)


def same(a, b):
    return (a == b).astype(jnp.int32)


def spread_rep(view, rep, shard, x, h, ssem, rsem):
    step = 1 - 2 * h
    xa = (x + step + XS) % XS
    xb = (x - step + XS) % XS
    xo = (x + 2) % XS
    ra, rb, partner = 2 * xa + h, 2 * xb + h, 2 * x + 1 - h
    mine = view(h, x)
    to_a = send(mine, mine, ssem.at[0], rsem.at[0], ra, shard)
    to_b = send(mine, mine, ssem.at[1], rsem.at[1], rb, shard)
    to_p = send(mine, mine, ssem.at[2], rsem.at[3], partner, shard)
    to_a.start()
    to_b.start()
    to_p.start()
    from_b, from_a, from_o = view(h, xb), view(h, xa), view(h, xo)
    pltpu.make_async_copy(from_b, from_b, rsem.at[0]).wait()
    on_a = send(from_b, from_b, ssem.at[3], rsem.at[2], ra, shard)
    on_p0 = send(from_b, from_b, ssem.at[4], rsem.at[4], partner, shard)
    on_a.start()
    on_p0.start()
    pltpu.make_async_copy(from_a, from_a, rsem.at[1]).wait()
    on_p1 = send(from_a, from_a, ssem.at[5], rsem.at[5], partner, shard)
    on_p1.start()
    pltpu.make_async_copy(from_o, from_o, rsem.at[2]).wait()
    on_p2 = send(from_o, from_o, ssem.at[6], rsem.at[6], partner, shard)
    on_p2.start()
    for index, col in ((3, x), (4, xa), (5, xb), (6, xo)):
        there = view(1 - h, col)
        pltpu.make_async_copy(there, there, rsem.at[index]).wait()
    for copy in (to_a, to_b, to_p, on_a, on_p0, on_p1, on_p2):
        copy.wait_send()


def gather_kernel(
    cell_of_slot, grads, g_out, own, pair, part, xin, red, mid, outb,
    own_sem, pair_sem, xs_sem, xr_sem, s1_sem, r1_sem, s2_sem, r2_sem, s3_sem, r3_sem,
):
    rep, shard, x, h = place()
    half = shard // HALF
    tile = shard % HALF
    partner = 2 * x + 1 - h
    barrier = pltpu.get_barrier_semaphore()

    load = pltpu.make_async_copy(grads.at[:, h], own, own_sem)
    load.start()

    def greet_source(r, carry):
        source = (HALF * r + tile) // TILES

        @pl.when(source != shard)
        def _():
            greet(barrier, rep, source)

        return carry

    lax.fori_loop(0, ROWB, greet_source, 0)

    def greet_half(r, carry):
        greet(barrier, rep, half * HALF + (tile + r) % HALF)
        return carry

    lax.fori_loop(1, HALF, greet_half, 0)
    greet(barrier, partner, shard)
    for d in range(1, XS):
        greet(barrier, 2 * ((x + d) % XS) + h, shard)
    waits = 2 * TILES + HALF - 1 + XS
    for i in range(TILES):
        waits = waits - same((TILES * shard + i) % HALF, tile)
    pl.semaphore_wait(barrier, waits)

    swap = send(grads.at[:, 1 - h], pair, pair_sem.at[0], pair_sem.at[1], partner, shard)
    swap.start()
    load.wait()
    swap.wait_recv()
    for q in range(XS):
        for c in range(COLB):
            lanes = slice(c * BLK + q * LANE, c * BLK + (q + 1) * LANE)
            part[q, :, c] = (own[:, :, lanes].astype(F32) + pair[:, :, lanes].astype(F32)).astype(BF)
    sends = []
    for d in range(1, XS):
        to = (x + d) % XS
        copy = send(part.at[to], xin.at[d - 1], xs_sem.at[d - 1], xr_sem.at[d - 1], 2 * to + h, shard)
        copy.start()
        sends.append(copy)
    for copy in sends:
        copy.wait_recv()
    red[...] = (
        (part[x].astype(F32) + xin[0].astype(F32)) + (xin[1].astype(F32) + xin[2].astype(F32))
    ).astype(BF)

    for i in range(TILES):
        u = TILES * shard + i
        for d in range(2):
            to = d * HALF + u % HALF
            dst = mid.at[pl.ds(COLB * (u // HALF), COLB)]

            @pl.when(to != shard)
            def _():
                send(red.at[i], dst, s1_sem.at[2 * i + d], r1_sem, rep, to).start()

            @pl.when(to == shard)
            def _():
                pltpu.make_async_copy(red.at[i], dst, r1_sem).start()

    pltpu.make_async_copy(mid, mid, r1_sem).wait()

    def pick(o, carry):
        for j in range(2):
            outb[o, j] = mid[cell_of_slot[2 * (half * HALF + o) + j]]
        to = half * HALF + o
        dst = g_out.at[tile, :, h, :, pl.ds(pl.multiple_of(x * LANE, LANE), LANE)]

        @pl.when(to != shard)
        def _():
            send(outb.at[o], dst, s2_sem.at[o], r2_sem, rep, to).start()

        @pl.when(to == shard)
        def _():
            pltpu.make_async_copy(outb.at[o], dst, r2_sem).start()

        return carry

    lax.fori_loop(0, HALF, pick, 0)

    def view(hh, col):
        return g_out.at[:, :, hh, :, pl.ds(pl.multiple_of(col * LANE, LANE), LANE)]

    mine = view(h, x)
    pltpu.make_async_copy(mine, mine, r2_sem).wait()
    spread_rep(view, rep, shard, x, h, s3_sem, r3_sem)

    swap.wait_send()
    for copy in sends:
        copy.wait_send()
    for i in range(TILES):
        u = TILES * shard + i
        for d in range(2):
            to = d * HALF + u % HALF

            @pl.when(to != shard)
            def _():
                send(red.at[i], red.at[i], s1_sem.at[2 * i + d], r1_sem, rep, to).wait_send()

    def drain(o, carry):
        to = half * HALF + o

        @pl.when(to != shard)
        def _():
            send(outb.at[o], outb.at[o], s2_sem.at[o], r2_sem, rep, to).wait_send()

        return carry

    lax.fori_loop(0, HALF, drain, 0)


def eye(size):
    row = lax.broadcasted_iota(jnp.int32, (size, size), 0)
    col = lax.broadcasted_iota(jnp.int32, (size, size), 1)
    return row == col


def mm(a, b):
    return jnp.dot(a, b, preferred_element_type=F32)


def root_less_one(new, scale):
    diag = eye(BLK)
    e = 0.25 * (jnp.where(diag, 1.0, 0.0) - new * (1.0 / scale))
    eb = e.astype(BF)
    u = 2.0 * e + mm(eb, eb)
    ub = u.astype(BF)
    v = 2.0 * u + mm(ub, ub)
    w = 4.0 * u - 5.0 * e
    z = (u - 0.25 * v) + 0.25 * mm(v.astype(BF), w.astype(BF))
    return z.astype(BF)


def work_kernel(live, g_in, left_prev, right_prev, left_new, right_new, p_out,
                lp, rp, ln, rn, pb, in_sem, out_sem):
    _, shard, x, h = place()
    loads = []
    for j in range(2):
        for src, dst, n in ((left_prev, lp, 0), (right_prev, rp, 1)):
            copy = pltpu.make_async_copy(src.at[j], dst.at[j], in_sem.at[2 * j + n])
            copy.start()
            loads.append(copy)
    stores = []
    for j in range(2):
        on = live[2 * shard + j] > 0
        g = g_in[:, j].reshape(BLK, BLK)
        g = jnp.where(on, g, jnp.zeros_like(g))
        gt = g.T
        diag = eye(BLK)
        roots = []
        for n, (prev, new, out, a, b) in enumerate(
            ((lp, ln, left_new, g, gt), (rp, rn, right_new, gt, g))
        ):
            loads[2 * j + n].wait()
            val = prev[j] + mm(a, b)
            val = jnp.where(on, val, jnp.zeros_like(val))
            new[j] = val
            copy = pltpu.make_async_copy(new.at[j], out.at[j], out_sem.at[2 * j + n])
            copy.start()
            stores.append(copy)
            scale = jnp.sum(jnp.where(diag, val, 0.0)) * (1.0 / BLK)
            scale = jnp.where(on, scale, 1.0)
            roots.append((root_less_one(val, scale), scale))
        (zl, cl), (zr, cr) = roots
        gf = g.astype(F32)
        y = lax.rsqrt(jnp.sqrt(jnp.full((8, LANE), cl, F32)))[0:1, 0:1] * (gf + mm(zl, g))
        p = lax.rsqrt(jnp.sqrt(jnp.full((8, LANE), cr, F32)))[0:1, 0:1] * (y + mm(y.astype(BF), zr))
        sg = jnp.full((8, LANE), jnp.sum(gf * gf), F32)
        sp = jnp.full((8, LANE), jnp.sum(p * p), F32)
        ratio = jnp.sqrt(sg / (sp + 1e-06))[0:1, 0:1]
        pb[...] = (p * ratio).astype(BF).reshape(HALF, 2, SUB, BLK)
        p_out[:, j] = pb[:, h, :, pl.ds(pl.multiple_of(x * LANE, LANE), LANE)]
    for copy in stores:
        copy.wait()


def return_kernel(
    slot_of_cell, p_in, d_out, mid, outb, land, full,
    s1_sem, r1_sem, s2_sem, r2_sem, s3_sem, r3_sem,
):
    rep, shard, x, h = place()
    half = shard // HALF
    tile = shard % HALF
    partner = 2 * x + 1 - h
    barrier = pltpu.get_barrier_semaphore()

    def greet_half(r, carry):
        greet(barrier, rep, half * HALF + (tile + r) % HALF)
        return carry

    lax.fori_loop(1, HALF, greet_half, 0)
    for i in range(TILES):
        for d in range(2):
            source = d * HALF + (TILES * shard + i) % HALF

            @pl.when(source != shard)
            def _():
                greet(barrier, rep, source)

    greet(barrier, partner, shard)
    greet(barrier, 2 * ((x + 1) % XS) + h, shard)
    greet(barrier, 2 * ((x + 3) % XS) + h, shard)
    waits = HALF - 1 + ROWB + 3
    for r in range(ROWB):
        waits = waits - same((HALF * r + tile) // TILES, shard)
    pl.semaphore_wait(barrier, waits)

    def give(k, carry):
        to = half * HALF + k
        dst = mid.at[pl.ds(2 * tile, 2)]

        @pl.when(to != shard)
        def _():
            send(p_in.at[k], dst, s1_sem.at[k], r1_sem, rep, to).start()

        @pl.when(to == shard)
        def _():
            pltpu.make_async_copy(p_in.at[k], dst, r1_sem).start()

        return carry

    lax.fori_loop(0, HALF, give, 0)
    pltpu.make_async_copy(mid, mid, r1_sem).wait()

    def pick(r, carry):
        for c in range(COLB):
            slot = slot_of_cell[COLB * r + c] - 2 * HALF * half
            inside = (slot >= 0) & (slot < 2 * HALF)
            value = mid[jnp.clip(slot, 0, 2 * HALF - 1)]
            outb[r, c] = jnp.where(inside, value, jnp.zeros_like(value))
        u = HALF * r + tile
        to = u // TILES
        dst = land.at[half, u % TILES]

        @pl.when(to != shard)
        def _():
            send(outb.at[r], dst, s2_sem.at[r], r2_sem, rep, to).start()

        @pl.when(to == shard)
        def _():
            pltpu.make_async_copy(outb.at[r], dst, r2_sem).start()

        return carry

    lax.fori_loop(0, ROWB, pick, 0)
    pltpu.make_async_copy(land, land, r2_sem).wait()

    def view(hh, col):
        return full.at[:, :, hh, :, pl.ds(pl.multiple_of(col * LANE, LANE), LANE)]

    for c in range(COLB):
        full[c, :, h, :, pl.ds(pl.multiple_of(x * LANE, LANE), LANE)] = land[0, :, c] + land[1, :, c]
    spread_rep(view, rep, shard, x, h, s3_sem, r3_sem)
    for c in range(COLB):
        d_out[:, :, :, c * BLK:(c + 1) * BLK] = full[c]

    def drain1(k, carry):
        to = half * HALF + k

        @pl.when(to != shard)
        def _():
            send(p_in.at[k], p_in.at[k], s1_sem.at[k], r1_sem, rep, to).wait_send()

        return carry

    lax.fori_loop(0, HALF, drain1, 0)

    def drain2(r, carry):
        to = (HALF * r + tile) // TILES

        @pl.when(to != shard)
        def _():
            send(outb.at[r], outb.at[r], s2_sem.at[r], r2_sem, rep, to).wait_send()

        return carry

    lax.fori_loop(0, ROWB, drain2, 0)


def tables(block_owner, block_row, block_col):
    count = block_owner.shape[0]
    index = jnp.arange(count, dtype=jnp.int32)
    earlier = (block_owner[:, None] == block_owner[None, :]) & (index[None, :] < index[:, None])
    slot = 2 * block_owner + jnp.sum(earlier.astype(jnp.int32), axis=1)
    cell = block_row // BLK * COLB + block_col // BLK
    at_slot = (slot[None, :] == jnp.arange(2 * SHARDS, dtype=jnp.int32)[:, None]).astype(jnp.int32)
    at_cell = (cell[None, :] == jnp.arange(CELLS, dtype=jnp.int32)[:, None]).astype(jnp.int32)
    cell_of_slot = jnp.sum(at_slot * cell[None, :], axis=1)
    live = jnp.sum(at_slot, axis=1)
    slot_of_cell = jnp.sum(at_cell * slot[None, :], axis=1)
    return cell_of_slot, live, slot_of_cell


SMEM = pl.BlockSpec(memory_space=pltpu.SMEM)
VMEM = pl.BlockSpec(memory_space=pltpu.VMEM)
ANY = pl.BlockSpec(memory_space=pl.ANY)
DMA = pltpu.SemaphoreType.DMA


def body(grads, left_prev, right_prev, block_owner, block_row, block_col):
    cell_of_slot, live, slot_of_cell = tables(block_owner, block_row, block_col)
    rows = grads.shape[1]
    gathered = pl.pallas_call(
        gather_kernel,
        out_shape=jax.ShapeDtypeStruct((HALF, 2, 2, SUB, BLK), BF),
        in_specs=[SMEM, ANY],
        out_specs=VMEM,
        scratch_shapes=[
            pltpu.VMEM((TILES, SUB, COLB * BLK), BF),
            pltpu.VMEM((TILES, SUB, COLB * BLK), BF),
            pltpu.VMEM((XS, TILES, COLB, SUB, LANE), BF),
            pltpu.VMEM((XS - 1, TILES, COLB, SUB, LANE), BF),
            pltpu.VMEM((TILES, COLB, SUB, LANE), BF),
            pltpu.VMEM((CELLS, SUB, LANE), BF),
            pltpu.VMEM((HALF, 2, SUB, LANE), BF),
            DMA, DMA((2,)), DMA((3,)), DMA((3,)), DMA((10,)), DMA, DMA((16,)), DMA, DMA((7,)), DMA((7,)),
        ],
        compiler_params=pltpu.CompilerParams(
            collective_id=0, has_side_effects=True, vmem_limit_bytes=32 * 1024 * 1024
        ),
        name="gather_blocks",
    )(cell_of_slot, grads.reshape(TILES, 2, SUB, COLB * BLK))

    sq = jax.ShapeDtypeStruct((2, BLK, BLK), F32)
    left_new, right_new, piece = pl.pallas_call(
        work_kernel,
        out_shape=(sq, sq, jax.ShapeDtypeStruct((HALF, 2, SUB, LANE), BF)),
        in_specs=[SMEM, VMEM, ANY, ANY],
        out_specs=(ANY, ANY, VMEM),
        scratch_shapes=[pltpu.VMEM((2, BLK, BLK), F32)] * 4
        + [pltpu.VMEM((HALF, 2, SUB, BLK), BF), DMA((4,)), DMA((4,))],
        compiler_params=pltpu.CompilerParams(vmem_limit_bytes=48 * 1024 * 1024),
        cost_estimate=pl.CostEstimate(flops=20 * 2 * BLK**3, bytes_accessed=8 * 2**20, transcendentals=0),
        name="precondition",
    )(live, gathered, left_prev, right_prev)

    direction = pl.pallas_call(
        return_kernel,
        out_shape=jax.ShapeDtypeStruct((TILES, 2, SUB, COLB * BLK), BF),
        in_specs=[SMEM, VMEM],
        out_specs=VMEM,
        scratch_shapes=[
            pltpu.VMEM((2 * HALF, SUB, LANE), BF),
            pltpu.VMEM((ROWB, COLB, SUB, LANE), BF),
            pltpu.VMEM((2, TILES, COLB, SUB, LANE), BF),
            pltpu.VMEM((COLB, TILES, 2, SUB, BLK), BF),
            DMA((16,)), DMA, DMA((10,)), DMA, DMA((7,)), DMA((7,)),
        ],
        compiler_params=pltpu.CompilerParams(
            collective_id=1, has_side_effects=True, vmem_limit_bytes=32 * 1024 * 1024
        ),
        name="return_blocks",
    )(slot_of_cell, piece)
    return direction.reshape(rows, COLB * BLK), left_new, right_new


def solution(mesh):
    in_specs = (P("rep", "shard", None), P("shard", None, None), P("shard", None, None), P(), P(), P())
    out_specs = (P("shard", None), P("shard", None, None), P("shard", None, None))
    return jax.shard_map(body, mesh=mesh, in_specs=in_specs, out_specs=out_specs, check_vma=False)
```

time: 695 us -> 85.5 us (0.12); the launches traced: 682 us -> 85.3 us
  waiting for transfers between devices: 441 us -> 0 us
  matrix products: 129 us -> 0 us
  Pallas kernels: 0 us -> 77.8 us
  local copies, waits for them, and re-layouts: 78.9 us -> 4.99 us
  between operations: 14.4 us -> 0.67 us
  other arithmetic: 12.4 us -> 1.82 us
    all_to_all x1 -> x0, waiting for transfers between devices: 236 us -> none  [body(): lax.all_to_all(spread, 'shard', split_axis=1, concat_axis=1, tiled=True)]
    all_gather x1 -> x0, waiting for transfers between devices: 135 us -> none  [body(): piece = lax.all_gather(total, 'shard', axis=0, tiled=True)]
    dot_general x11 -> x0, matrix products: 129 us -> none  [the longest x1 48.2 us: body(): jnp.einsum('sc,rck->srk', col_pick, piece3, preferred_element_type=jnp.fl...]
    pallas_call x0 -> x3, Pallas kernels: none -> 77.8 us  [the longest x1 41.5 us: body(): pl.pallas_call(gather_kernel, out_shape=jax.ShapeDtypeStruct((HALF, 2, 2,...]
    psum x1 -> x0, waiting for transfers between devices: 69.8 us -> none  [body(): total = lax.psum(grads[0].astype(jnp.float32).astype(jnp.bfloat16), 'rep')]
    mul x4 -> x0, local copies, waits for them, and re-layouts: 35.8 us -> none  [body(): row_pick.astype(jnp.bfloat16)[:, :, None, None] * dir_blocks[:, None, :, :]]
    dot_general x1 -> x0, local copies, waits for them, and re-layouts: 20.7 us -> none  [body(): jnp.einsum('sc,rck->srk', col_pick, piece3, preferred_element_type=jnp.fl...]
    all_gather x1 -> x0, local copies, waits for them, and re-layouts: 20.7 us -> none  [body(): piece = lax.all_gather(total, 'shard', axis=0, tiled=True)]
  transfers between devices with their start and end apart: 3 -> 0, of which waited for: 3 -> 0; matrix products, arithmetic and copies ran while one was open for 1% -> 0% of each run, Pallas kernels for 0% -> 0%
where the time goes in v1:
time: 85.5 us; the launch traced here: 85.3 us
  Pallas kernels  77.8 us (91%)
  local copies, waits for them, and re-layouts  4.99 us (6%)
  other arithmetic  1.82 us (2%)
    pallas_call x1, Pallas kernels, body(): pl.pallas_call(gather_kernel, out_shape=jax.ShapeDtypeStruct((HALF, 2, 2,...  41.5 us
    pallas_call x1, Pallas kernels, body(): pl.pallas_call(return_kernel, out_shape=jax.ShapeDtypeStruct((TILES, 2, S...  25.9 us
    pallas_call x1, Pallas kernels, body(): pl.pallas_call(work_kernel, out_shape=(sq, sq, jax.ShapeDtypeStruct((HALF...  10.4 us
    unnamed x7, local copies, waits for them, and re-layouts  4.99 us

profile of v1, /device:TPU:1, one launch (start us, length us, event | category | flops | bytes accessed | tf_op | source)
XLA Modules:
  0.0 85.3 jit_solution(12010672501664526354)
XLA Ops:
  0.6 0.9 %convert_reduce_fusion.1 = s32[30]{0:T(128)S(1)} fusion(s32[30]{0:T(128)} %param.9), kind=kLoop, calls=%fused_computation.4 | loop fusion | flops 4470 | bytes 240 | tf_op jit(solution)/shard_map/reduce_sum | solution.py:376
  1.5 0.7 multiply_add_fusion
  2.2 0.1 select_reduce_fusion.1.slot_of_cell
  2.4 0.1 select_reduce_fusion
  2.5 0.0 copy-start
  2.5 1.0 %copy-done = bf16[1,160,1536]{2,1,0:T(8,128)(2,1)S(1)} copy-done((bf16[1,160,1536]{2,1,0:T(8,128)(2,1)S(1)}, bf16[1,160,1536]{2,1,0:T(8,128)(2,1)}, u32[]{:S(2)}) %copy-start) | copy-done | bytes 491544
  3.5 41.5 %gather_blocks.1.g_in = bf16[16,2,2,16,512]{4,3,2,1,0:T(8,128)(2,1)S(1)} custom-call(s32[64]{0:T(128)S(1)} %get-tuple-element.9.cell_of_slot, bf16[5,2,16,1536]{3,2,1,0:T(8,128)(2,1)S(1)} %bitcast.3), custom_call_target="tpu_custom_call" | custom-call | tf_op jit(solution)/shard_map/gather_blocks/pallas_call | solution.py:395
  45.0 0.0 copy-start.1
  45.0 1.6 %copy-done.1 = f32[2,512,512]{2,1,0:T(8,128)S(1)} copy-done((f32[2,512,512]{2,1,0:T(8,128)S(1)}, f32[2,512,512]{2,1,0:T(8,128)}, u32[]{:S(2)}) %copy-start.1) | copy-done | bytes 2097176
  46.6 0.0 copy-start.2
  46.6 1.6 %copy-done.2 = f32[2,512,512]{2,1,0:T(8,128)S(1)} copy-done((f32[2,512,512]{2,1,0:T(8,128)S(1)}, f32[2,512,512]{2,1,0:T(8,128)}, u32[]{:S(2)}) %copy-start.2) | copy-done | bytes 2097176
  48.2 10.4 %precondition.1 = (f32[2,512,512]{2,1,0:T(8,128)}, f32[2,512,512]{2,1,0:T(8,128)}, bf16[16,2,16,128]{3,2,1,0:T(8,128)(2,1)S(1)}) custom-call(s32[64]{0:T(128)S(1)} %get-tuple-element.10.live, bf16[16,2,2,16,512]{4,3,2,1,0:T(8,128)(2,1)S(1)} %gather_blocks.1.g_in, f32[2,512,512]{2,1,0:T(8,128)S(1)} %copy-done.1, f32[2,512,512]{2,1,0:T(8,128)S(1)} %copy-done.2), custom_call_target="tpu_custom_call" | custom-call | flops 5368709120 | bytes 8388608 | tf_op jit(solution)/shard_map/precondition/pallas_call | solution.py:417
  58.6 25.9 %return_blocks.1 = bf16[5,2,16,1536]{3,2,1,0:T(8,128)(2,1)S(1)} custom-call(s32[30]{0:T(128)S(1)} %select_reduce_fusion.1.slot_of_cell, bf16[16,2,16,128]{3,2,1,0:T(8,128)(2,1)S(1)} %get-tuple-element.6.p_in), custom_call_target="tpu_custom_call" | custom-call | tf_op jit(solution)/shard_map/return_blocks/pallas_call | solution.py:429
  84.5 0.8 copy.10
Async XLA Ops:
  2.5 1.0 %copy-start = (bf16[1,160,1536]{2,1,0:T(8,128)(2,1)S(1)}, bf16[1,160,1536]{2,1,0:T(8,128)(2,1)}, u32[]{:S(2)}) copy-start(bf16[1,160,1536]{2,1,0:T(8,128)(2,1)} %param.6) | copy-start | bytes 1474564
  45.0 1.6 %copy-start.1 = (f32[2,512,512]{2,1,0:T(8,128)S(1)}, f32[2,512,512]{2,1,0:T(8,128)}, u32[]{:S(2)}) copy-start(f32[2,512,512]{2,1,0:T(8,128)} %left_prev.1) | copy-start | bytes 6291460
  46.6 1.6 %copy-start.2 = (f32[2,512,512]{2,1,0:T(8,128)S(1)}, f32[2,512,512]{2,1,0:T(8,128)}, u32[]{:S(2)}) copy-start(f32[2,512,512]{2,1,0:T(8,128)} %right_prev.1) | copy-start | bytes 6291460

commit v2 on v1

v2 whole, which is shorter than its diff:
```python
import jax
import jax.numpy as jnp
from jax import lax
from jax.experimental import pallas as pl
from jax.experimental.pallas import tpu as pltpu
from jax.sharding import PartitionSpec as P

BLK = 512
COLB = 3
ROWB = 10
CELLS = 30
SHARDS = 32
HALF = 16
TILES = 5
LANE = 128
SUB = 16
XS = 4
MESH = pl.DeviceIdType.MESH
BF = jnp.bfloat16
F32 = jnp.float32


def place():
    rep = lax.axis_index("rep")
    shard = lax.axis_index("shard")
    x = rep // 2
    h = rep % 2
    return rep, shard, x, h


def send(src, dst, send_sem, recv_sem, rep, shard):
    return pltpu.make_async_remote_copy(
        src_ref=src,
        dst_ref=dst,
        send_sem=send_sem,
        recv_sem=recv_sem,
        device_id=(rep, shard),
        device_id_type=MESH,
    )


def greet(barrier, rep, shard):
    pl.semaphore_signal(barrier, inc=1, device_id=(rep, shard), device_id_type=MESH)


def same(a, b):
    return (a == b).astype(jnp.int32)


def spread_rep(view, rep, shard, x, h, ssem, rsem):
    partner = 2 * x + 1 - h
    mine = view(h, x)
    copies = []
    for n in (2, 1, 3):
        to = 2 * ((x + n) % XS) + h
        copies.append(send(mine, mine, ssem.at[n], rsem.at[n], to, shard))
    copies.append(send(mine, mine, ssem.at[0], rsem.at[0], partner, shard))
    for copy in copies:
        copy.start()
    for n in (1, 3, 2):
        piece = view(h, (x + XS - n) % XS)
        pltpu.make_async_copy(piece, piece, rsem.at[n]).wait()
        copy = send(piece, piece, ssem.at[3 + n], rsem.at[3 + n], partner, shard)
        copy.start()
        copies.append(copy)
    for index, n in ((0, 0), (4, 1), (6, 3), (5, 2)):
        there = view(1 - h, (x + XS - n) % XS)
        pltpu.make_async_copy(there, there, rsem.at[index]).wait()
    for copy in copies:
        copy.wait_send()


def eye(size):
    row = lax.broadcasted_iota(jnp.int32, (size, size), 0)
    col = lax.broadcasted_iota(jnp.int32, (size, size), 1)
    return row == col


def mm(a, b):
    return jnp.dot(a, b, preferred_element_type=F32)


def root_less_one(new, scale):
    diag = eye(BLK)
    e = 0.25 * (jnp.where(diag, 1.0, 0.0) - new * (1.0 / scale))
    eb = e.astype(BF)
    u = 2.0 * e + mm(eb, eb)
    ub = u.astype(BF)
    v = 2.0 * u + mm(ub, ub)
    w = 4.0 * u - 5.0 * e
    z = (u - 0.25 * v) + 0.25 * mm(v.astype(BF), w.astype(BF))
    return z.astype(BF)


def step_kernel(
    cell_of_slot, live, slot_of_cell, grads, left_prev, right_prev, d_out, g_out,
    own, pair, part, xin, red, mid, outb, lp, rp, pb, p_in, mid_b, outb_b, land, full,
    own_sem, pair_sem, xs_sem, xr_sem, s1_sem, r1_sem, s2_sem, r2_sem, s3_sem, r3_sem, in_sem,
    s4_sem, r4_sem, s5_sem, r5_sem, s6_sem, r6_sem,
):
    rep, shard, x, h = place()
    half = shard // HALF
    tile = shard % HALF
    partner = 2 * x + 1 - h
    barrier = pltpu.get_barrier_semaphore()

    load = pltpu.make_async_copy(grads.at[:, h], own, own_sem)
    load.start()
    loads = []
    for j in range(2):
        for src, dst, n in ((left_prev, lp, 0), (right_prev, rp, 1)):
            copy = pltpu.make_async_copy(src.at[j], dst.at[j], in_sem.at[2 * j + n])
            copy.start()
            loads.append(copy)

    def greet_source(r, carry):
        source = (HALF * r + tile) // TILES

        @pl.when(source != shard)
        def _():
            greet(barrier, rep, source)

        return carry

    lax.fori_loop(0, ROWB, greet_source, 0)

    def greet_half(r, carry):
        greet(barrier, rep, half * HALF + (tile + r) % HALF)
        return carry

    lax.fori_loop(1, HALF, greet_half, 0)
    for i in range(TILES):
        for d in range(2):
            source = d * HALF + (TILES * shard + i) % HALF

            @pl.when(source != shard)
            def _():
                greet(barrier, rep, source)

    greet(barrier, partner, shard)
    for d in range(1, XS):
        greet(barrier, 2 * ((x + d) % XS) + h, shard)
    waits = 2 * TILES + HALF - 1 + XS + ROWB
    for i in range(TILES):
        waits = waits - same((TILES * shard + i) % HALF, tile)
    for r in range(ROWB):
        waits = waits - same((HALF * r + tile) // TILES, shard)
    pl.semaphore_wait(barrier, waits)

    swap = send(grads.at[:, 1 - h], pair, pair_sem.at[0], pair_sem.at[1], partner, shard)
    swap.start()
    load.wait()
    swap.wait_recv()
    for q in range(XS):
        for c in range(COLB):
            lanes = slice(c * BLK + q * LANE, c * BLK + (q + 1) * LANE)
            part[q, :, c] = (own[:, :, lanes].astype(F32) + pair[:, :, lanes].astype(F32)).astype(BF)
    sends = []
    for d in range(1, XS):
        to = (x + d) % XS
        copy = send(part.at[to], xin.at[d - 1], xs_sem.at[d - 1], xr_sem.at[d - 1], 2 * to + h, shard)
        copy.start()
        sends.append(copy)
    for copy in sends:
        copy.wait_recv()
    red[...] = (
        (part[x].astype(F32) + xin[0].astype(F32)) + (xin[1].astype(F32) + xin[2].astype(F32))
    ).astype(BF)

    for i in range(TILES):
        u = TILES * shard + i
        for d in range(2):
            to = d * HALF + u % HALF
            dst = mid.at[pl.ds(COLB * (u // HALF), COLB)]

            @pl.when(to != shard)
            def _():
                send(red.at[i], dst, s1_sem.at[2 * i + d], r1_sem, rep, to).start()

            @pl.when(to == shard)
            def _():
                pltpu.make_async_copy(red.at[i], dst, r1_sem).start()

    pltpu.make_async_copy(mid, mid, r1_sem).wait()

    def pick(o, carry):
        for j in range(2):
            outb[o, j] = mid[cell_of_slot[2 * (half * HALF + o) + j]]
        to = half * HALF + o
        dst = g_out.at[tile, :, h, :, pl.ds(pl.multiple_of(x * LANE, LANE), LANE)]

        @pl.when(to != shard)
        def _():
            send(outb.at[o], dst, s2_sem.at[o], r2_sem, rep, to).start()

        @pl.when(to == shard)
        def _():
            pltpu.make_async_copy(outb.at[o], dst, r2_sem).start()

        return carry

    lax.fori_loop(0, HALF, pick, 0)

    def view(hh, col):
        return g_out.at[:, :, hh, :, pl.ds(pl.multiple_of(col * LANE, LANE), LANE)]

    mine = view(h, x)
    pltpu.make_async_copy(mine, mine, r2_sem).wait()
    spread_rep(view, rep, shard, x, h, s3_sem, r3_sem)

    swap.wait_send()
    for copy in sends:
        copy.wait_send()
    for i in range(TILES):
        u = TILES * shard + i
        for d in range(2):
            to = d * HALF + u % HALF

            @pl.when(to != shard)
            def _():
                send(red.at[i], red.at[i], s1_sem.at[2 * i + d], r1_sem, rep, to).wait_send()

    def drain(o, carry):
        to = half * HALF + o

        @pl.when(to != shard)
        def _():
            send(outb.at[o], outb.at[o], s2_sem.at[o], r2_sem, rep, to).wait_send()

        return carry

    lax.fori_loop(0, HALF, drain, 0)

    for j in range(2):
        on = live[2 * shard + j] > 0
        g = g_out[:, j].reshape(BLK, BLK)
        g = jnp.where(on, g, jnp.zeros_like(g))
        gt = g.T
        diag = eye(BLK)
        roots = []
        for n, (prev, a, b) in enumerate(((lp, g, gt), (rp, gt, g))):
            loads[2 * j + n].wait()
            val = prev[j] + mm(a, b)
            val = jnp.where(on, val, jnp.zeros_like(val))
            scale = jnp.sum(jnp.where(diag, val, 0.0)) * (1.0 / BLK)
            scale = jnp.where(on, scale, 1.0)
            roots.append((root_less_one(val, scale), scale))
        (zl, cl), (zr, cr) = roots
        gf = g.astype(F32)
        y = lax.rsqrt(jnp.sqrt(jnp.full((8, LANE), cl, F32)))[0:1, 0:1] * (gf + mm(zl, g))
        p = lax.rsqrt(jnp.sqrt(jnp.full((8, LANE), cr, F32)))[0:1, 0:1] * (y + mm(y.astype(BF), zr))
        sg = jnp.full((8, LANE), jnp.sum(gf * gf), F32)
        sp = jnp.full((8, LANE), jnp.sum(p * p), F32)
        ratio = jnp.sqrt(sg / (sp + 1e-06))[0:1, 0:1]
        pb[...] = (p * ratio).astype(BF).reshape(HALF, 2, SUB, BLK)
        p_in[:, j] = pb[:, h, :, pl.ds(pl.multiple_of(x * LANE, LANE), LANE)]

    def give(k, carry):
        to = half * HALF + k
        dst = mid_b.at[pl.ds(2 * tile, 2)]

        @pl.when(to != shard)
        def _():
            send(p_in.at[k], dst, s4_sem.at[k], r4_sem, rep, to).start()

        @pl.when(to == shard)
        def _():
            pltpu.make_async_copy(p_in.at[k], dst, r4_sem).start()

        return carry

    lax.fori_loop(0, HALF, give, 0)
    pltpu.make_async_copy(mid_b, mid_b, r4_sem).wait()

    def pick_cells(r, carry):
        for c in range(COLB):
            slot = slot_of_cell[COLB * r + c] - 2 * HALF * half
            inside = (slot >= 0) & (slot < 2 * HALF)
            value = mid_b[jnp.clip(slot, 0, 2 * HALF - 1)]
            outb_b[r, c] = jnp.where(inside, value, jnp.zeros_like(value))
        u = HALF * r + tile
        to = u // TILES
        dst = land.at[half, u % TILES]

        @pl.when(to != shard)
        def _():
            send(outb_b.at[r], dst, s5_sem.at[r], r5_sem, rep, to).start()

        @pl.when(to == shard)
        def _():
            pltpu.make_async_copy(outb_b.at[r], dst, r5_sem).start()

        return carry

    lax.fori_loop(0, ROWB, pick_cells, 0)
    pltpu.make_async_copy(land, land, r5_sem).wait()

    def view_d(hh, col):
        return full.at[:, :, hh, :, pl.ds(pl.multiple_of(col * LANE, LANE), LANE)]

    for c in range(COLB):
        full[c, :, h, :, pl.ds(pl.multiple_of(x * LANE, LANE), LANE)] = land[0, :, c] + land[1, :, c]
    spread_rep(view_d, rep, shard, x, h, s6_sem, r6_sem)
    for c in range(COLB):
        d_out[:, :, :, c * BLK:(c + 1) * BLK] = full[c]

    def drain1(k, carry):
        to = half * HALF + k

        @pl.when(to != shard)
        def _():
            send(p_in.at[k], p_in.at[k], s4_sem.at[k], r4_sem, rep, to).wait_send()

        return carry

    lax.fori_loop(0, HALF, drain1, 0)

    def drain2(r, carry):
        to = (HALF * r + tile) // TILES

        @pl.when(to != shard)
        def _():
            send(outb_b.at[r], outb_b.at[r], s5_sem.at[r], r5_sem, rep, to).wait_send()

        return carry

    lax.fori_loop(0, ROWB, drain2, 0)


def factors_kernel(live, g_in, left_prev, right_prev, left_new, right_new, lp, rp, ln, rn, in_sem, out_sem):
    shard = lax.axis_index("shard")
    loads = []
    for j in range(2):
        for src, dst, n in ((left_prev, lp, 0), (right_prev, rp, 1)):
            copy = pltpu.make_async_copy(src.at[j], dst.at[j], in_sem.at[2 * j + n])
            copy.start()
            loads.append(copy)
    stores = []
    for j in range(2):
        on = live[2 * shard + j] > 0
        g = g_in[:, j].reshape(BLK, BLK)
        g = jnp.where(on, g, jnp.zeros_like(g))
        gt = g.T
        for n, (prev, new, out, a, b) in enumerate(
            ((lp, ln, left_new, g, gt), (rp, rn, right_new, gt, g))
        ):
            prod = mm(a, b)
            loads[2 * j + n].wait()
            new[j] = jnp.where(on, prev[j] + prod, 0.0)
            copy = pltpu.make_async_copy(new.at[j], out.at[j], out_sem.at[2 * j + n])
            copy.start()
            stores.append(copy)
    for copy in stores:
        copy.wait()


def tables(block_owner, block_row, block_col):
    count = block_owner.shape[0]
    index = jnp.arange(count, dtype=jnp.int32)
    earlier = (block_owner[:, None] == block_owner[None, :]) & (index[None, :] < index[:, None])
    slot = 2 * block_owner + jnp.sum(earlier.astype(jnp.int32), axis=1)
    cell = block_row // BLK * COLB + block_col // BLK
    at_slot = (slot[None, :] == jnp.arange(2 * SHARDS, dtype=jnp.int32)[:, None]).astype(jnp.int32)
    at_cell = (cell[None, :] == jnp.arange(CELLS, dtype=jnp.int32)[:, None]).astype(jnp.int32)
    cell_of_slot = jnp.sum(at_slot * cell[None, :], axis=1)
    live = jnp.sum(at_slot, axis=1)
    slot_of_cell = jnp.sum(at_cell * slot[None, :], axis=1)
    return cell_of_slot, live, slot_of_cell


SMEM = pl.BlockSpec(memory_space=pltpu.SMEM)
VMEM = pl.BlockSpec(memory_space=pltpu.VMEM)
ANY = pl.BlockSpec(memory_space=pl.ANY)
DMA = pltpu.SemaphoreType.DMA


def body(grads, left_prev, right_prev, block_owner, block_row, block_col):
    cell_of_slot, live, slot_of_cell = tables(block_owner, block_row, block_col)
    rows = grads.shape[1]
    direction, gathered = pl.pallas_call(
        step_kernel,
        out_shape=(
            jax.ShapeDtypeStruct((TILES, 2, SUB, COLB * BLK), BF),
            jax.ShapeDtypeStruct((HALF, 2, 2, SUB, BLK), BF),
        ),
        in_specs=[SMEM, SMEM, SMEM, ANY, ANY, ANY],
        out_specs=(VMEM, VMEM),
        scratch_shapes=[
            pltpu.VMEM((TILES, SUB, COLB * BLK), BF),
            pltpu.VMEM((TILES, SUB, COLB * BLK), BF),
            pltpu.VMEM((XS, TILES, COLB, SUB, LANE), BF),
            pltpu.VMEM((XS - 1, TILES, COLB, SUB, LANE), BF),
            pltpu.VMEM((TILES, COLB, SUB, LANE), BF),
            pltpu.VMEM((CELLS, SUB, LANE), BF),
            pltpu.VMEM((HALF, 2, SUB, LANE), BF),
            pltpu.VMEM((2, BLK, BLK), F32),
            pltpu.VMEM((2, BLK, BLK), F32),
            pltpu.VMEM((HALF, 2, SUB, BLK), BF),
            pltpu.VMEM((HALF, 2, SUB, LANE), BF),
            pltpu.VMEM((2 * HALF, SUB, LANE), BF),
            pltpu.VMEM((ROWB, COLB, SUB, LANE), BF),
            pltpu.VMEM((2, TILES, COLB, SUB, LANE), BF),
            pltpu.VMEM((COLB, TILES, 2, SUB, BLK), BF),
            DMA, DMA((2,)), DMA((3,)), DMA((3,)), DMA((10,)), DMA, DMA((16,)), DMA, DMA((7,)), DMA((7,)), DMA((4,)),
            DMA((16,)), DMA, DMA((10,)), DMA, DMA((7,)), DMA((7,)),
        ],
        compiler_params=pltpu.CompilerParams(
            collective_id=0, has_side_effects=True, vmem_limit_bytes=58 * 1024 * 1024
        ),
        name="shampoo_step",
    )(cell_of_slot, live, slot_of_cell, grads.reshape(TILES, 2, SUB, COLB * BLK), left_prev, right_prev)

    sq = jax.ShapeDtypeStruct((2, BLK, BLK), F32)
    left_new, right_new = pl.pallas_call(
        factors_kernel,
        out_shape=(sq, sq),
        in_specs=[SMEM, VMEM, ANY, ANY],
        out_specs=(ANY, ANY),
        scratch_shapes=[pltpu.VMEM((2, BLK, BLK), F32)] * 4 + [DMA((4,)), DMA((4,))],
        compiler_params=pltpu.CompilerParams(vmem_limit_bytes=58 * 1024 * 1024),
        cost_estimate=pl.CostEstimate(flops=4 * 2 * BLK**3, bytes_accessed=8 * 2**20, transcendentals=0),
        name="new_factors",
    )(live, gathered, left_prev, right_prev)
    return direction.reshape(rows, COLB * BLK), left_new, right_new


def solution(mesh):
    in_specs = (P("rep", "shard", None), P("shard", None, None), P("shard", None, None), P(), P(), P())
    out_specs = (P("shard", None), P("shard", None, None), P("shard", None, None))
    return jax.shard_map(body, mesh=mesh, in_specs=in_specs, out_specs=out_specs, check_vma=False)
```

time: 85.5 us -> 80.6 us (0.943)
  local copies, waits for them, and re-layouts: 4.99 us -> 0.79 us
  Pallas kernels: 77.8 us -> 76.2 us
  other arithmetic: 1.82 us -> 2.84 us
    unnamed x7 -> x3, local copies, waits for them, and re-layouts: 4.99 us -> 0.79 us
    pallas_call x3 -> x2, Pallas kernels: 77.8 us -> 76.2 us  [the longest x1 70.6 us: body(): pl.pallas_call(step_kernel, out_shape=(jax.ShapeDtypeStruct((TILES, 2, SU...]
where the time goes in v2:
time: 80.6 us; the launch traced here: 80.5 us
  Pallas kernels  76.2 us (95%)
  other arithmetic  2.84 us (4%)
    pallas_call x1, Pallas kernels, body(): pl.pallas_call(step_kernel, out_shape=(jax.ShapeDtypeStruct((TILES, 2, SU...  70.6 us
    pallas_call x1, Pallas kernels, body(): pl.pallas_call(factors_kernel, out_shape=(sq, sq), in_specs=[SMEM, VMEM,...  5.59 us

profile of v2, /device:TPU:1, one launch (start us, length us, event | category | flops | bytes accessed | tf_op | source)
XLA Modules:
  0.0 80.5 jit_solution(2810237791514328154)
XLA Ops:
  0.6 0.9 %convert_reduce_fusion.1 = s32[30]{0:T(128)S(1)} fusion(s32[30]{0:T(128)} %param.9), kind=kLoop, calls=%fused_computation.5 | loop fusion | flops 4470 | bytes 240 | tf_op jit(solution)/shard_map/reduce_sum | solution.py:361
  1.5 0.7 fusion.1
  2.2 0.6 select_reduce_fusion.slot_of_cell
  2.9 0.6 convert_reduce_fusion
  3.5 70.6 %shampoo_step.1 = (bf16[5,2,16,1536]{3,2,1,0:T(8,128)(2,1)}, bf16[16,2,2,16,512]{4,3,2,1,0:T(8,128)(2,1)}) custom-call(s32[64]{0:T(128)} %get-tuple-element.12.cell_of_slot, s32[64]{0:T(128)} %get-tuple-element.11.live, s32[30]{0:T(128)} %select_reduce_fusion.slot_of_cell, bf16[5,2,16,1536]{3,2,1,0:T(8,128)(2,1)} %bitcast.3, f32[2,512,512]{2,1,0:T(8,128)} %left_prev.3, ...), custom_call_target="tpu_custom_call" | custom-call | tf_op jit(solution)/shard_map/shampoo_step/pallas_call | solution.py:380
  74.1 0.0 copy-start
  74.1 5.6 %new_factors.1 = (f32[2,512,512]{2,1,0:T(8,128)}, f32[2,512,512]{2,1,0:T(8,128)}) custom-call(s32[64]{0:T(128)} %get-tuple-element.11.live, bf16[16,2,2,16,512]{4,3,2,1,0:T(8,128)(2,1)} %get-tuple-element.8.g_in, f32[2,512,512]{2,1,0:T(8,128)} %left_prev.3, f32[2,512,512]{2,1,0:T(8,128)} %right_prev.3), custom_call_target="tpu_custom_call" | custom-call | flops 1073741824 | bytes 8388608 | tf_op jit(solution)/shard_map/new_factors/pallas_call | solution.py:414
  79.7 0.0 copy-done
  79.7 0.8 copy.10
Async XLA Ops:
  74.1 5.6 %copy-start = (bf16[5,2,16,1536]{3,2,1,0:T(8,128)(2,1)S(1)}, bf16[5,2,16,1536]{3,2,1,0:T(8,128)(2,1)}, u32[]{:S(2)}) copy-start(bf16[5,2,16,1536]{3,2,1,0:T(8,128)(2,1)} %get-tuple-element.7) | copy-start | bytes 1474564

commit v3 on v2

v3 whole, which is shorter than its diff:
```python
import jax
import jax.numpy as jnp
from jax import lax
from jax.experimental import pallas as pl
from jax.experimental.pallas import tpu as pltpu
from jax.sharding import PartitionSpec as P

BLK = 512
COLB = 3
ROWB = 10
CELLS = 30
SHARDS = 32
HALF = 16
TILES = 5
LANE = 128
SUB = 16
XS = 4
MESH = pl.DeviceIdType.MESH
BF = jnp.bfloat16
F32 = jnp.float32


def place():
    rep = lax.axis_index("rep")
    shard = lax.axis_index("shard")
    x = rep // 2
    h = rep % 2
    return rep, shard, x, h


def send(src, dst, send_sem, recv_sem, rep, shard):
    return pltpu.make_async_remote_copy(
        src_ref=src,
        dst_ref=dst,
        send_sem=send_sem,
        recv_sem=recv_sem,
        device_id=(rep, shard),
        device_id_type=MESH,
    )


def greet(barrier, rep, shard):
    pl.semaphore_signal(barrier, inc=1, device_id=(rep, shard), device_id_type=MESH)


def eye(size):
    row = lax.broadcasted_iota(jnp.int32, (size, size), 0)
    col = lax.broadcasted_iota(jnp.int32, (size, size), 1)
    return row == col


def mm(a, b):
    return jnp.dot(a, b, preferred_element_type=F32)


def root_less_one(new, scale):
    diag = eye(BLK)
    e = 0.25 * (jnp.where(diag, 1.0, 0.0) - new * (1.0 / scale))
    eb = e.astype(BF)
    u = 2.0 * e + mm(eb, eb)
    ub = u.astype(BF)
    v = 2.0 * u + mm(ub, ub)
    w = 4.0 * u - 5.0 * e
    z = (u - 0.25 * v) + 0.25 * mm(v.astype(BF), w.astype(BF))
    return z.astype(BF)


def step_kernel(
    cell_of_slot, slot_of_cell, grads, left_prev, right_prev, d_out, g_own,
    own, pair, part, xin, red, pvf, pvb, pm, po, pv, gc, mid, outb, acc, zb, scl, pb, full,
    own_sem, pvf_sem, pair_sem, xs_sem, xr_sem, p1_sem, p1r_sem, p2_sem, p2r_sem, gs_sem, gr_sem, ge_sem,
    t1_sem, t1r_sem, t2_sem, t2r_sem, os_sem, or_sem, z_sem, ss_sem, sr_sem, ds_sem, dr_sem, ready,
):
    rep = lax.axis_index("rep")
    shard = lax.axis_index("shard")
    x = rep // 2
    h = rep % 2
    half = shard // HALF
    w = shard % HALF
    r = w // 3
    j = w % 3
    partner = 2 * x + 1 - h
    summing = x < COLB
    home = summing & (j == 1)
    passing = half == h
    lanes = pl.ds(pl.multiple_of(x * LANE, LANE), LANE)
    barrier = pltpu.get_barrier_semaphore()

    def pass_on(src, dst, send_sem, recv_sem, to_rep, to_shard):
        me = (to_rep == rep) & (to_shard == shard)

        @pl.when(jnp.logical_not(me))
        def _():
            send(src, dst, send_sem, recv_sem, to_rep, to_shard).start()

        @pl.when(me)
        def _():
            pltpu.make_async_copy(src, dst, recv_sem).start()

    def passed(src, send_sem, recv_sem, to_rep, to_shard):
        me = (to_rep == rep) & (to_shard == shard)

        @pl.when(jnp.logical_not(me))
        def _():
            send(src, src, send_sem, recv_sem, to_rep, to_shard).wait_send()

    def arrived(ref, sem):
        pltpu.make_async_copy(ref, ref, sem).wait()

    def loop(count, fn):
        def step(n, carry):
            fn(n)
            return carry

        lax.fori_loop(0, count, step, 0)

    load = pltpu.make_async_copy(grads.at[:, h], own, own_sem)
    load.start()

    @pl.when(h == 0)
    def _():
        pltpu.make_async_copy(left_prev.at[:, :, :, lanes], pvf, pvf_sem).start()

    @pl.when(h == 1)
    def _():
        pltpu.make_async_copy(right_prev.at[:, :, :, lanes], pvf, pvf_sem).start()

    loop(SHARDS - 1, lambda n: greet(barrier, rep, (shard + 1 + n) % SHARDS))
    for n in range(1, XS):
        greet(barrier, 2 * ((x + n) % XS) + h, shard)
    greet(barrier, partner, shard)
    arrived(pvf, pvf_sem)
    for n in range(2):
        pvb[:, n] = pvf[n].astype(BF)
    pl.semaphore_wait(barrier, SHARDS - 1 + XS)

    swap = send(grads.at[:, 1 - h], pair, pair_sem.at[0], pair_sem.at[1], partner, shard)
    swap.start()
    for n in range(1, XS):
        pl.semaphore_signal(
            ready, inc=1, device_id=(2 * ((x + n) % XS) + h, shard), device_id_type=MESH
        )
    mine = pm.at[pl.ds(2 * shard, 2)]
    loop(SHARDS, lambda t: pass_on(pvb.at[t], mine, p1_sem.at[t], p1r_sem, rep, t))

    load.wait()
    swap.wait_recv()
    for c in range(COLB):
        cols = slice(c * BLK, (c + 1) * BLK)
        part[c] = (own[:, :, cols].astype(F32) + pair[:, :, cols].astype(F32)).astype(BF)
    for c in range(COLB):

        @pl.when(x != c)
        def _():
            n = (c - x + XS) % XS - 1
            send(part.at[c], xin.at[n], xs_sem.at[c], xr_sem.at[n], 2 * c + h, shard).start()

    arrived(pm, p1r_sem)
    pl.semaphore_wait(ready, XS - 1)
    tile_at_home = pv.at[shard, :, lanes]

    def home_of(cell):
        row = cell // COLB
        return 2 * (cell % COLB) + h, HALF * (row // 5) + 3 * (row % 5) + 1

    def give_factor(cell):
        po[cell] = pm[slot_of_cell[cell]]
        to_rep, to_shard = home_of(cell)
        pass_on(po.at[cell], tile_at_home, p2_sem.at[cell], p2r_sem, to_rep, to_shard)

    loop(CELLS, give_factor)

    def to_homes(act):
        @pl.when(j == 2)
        def _():
            act(0, red, gc.at[pl.ds(10 - r, TILES), h], shard - 1)

        for n in range(6):

            @pl.when((j == 0) & (r == n))
            def _():
                if n > 0:
                    act(0, red.at[0:n], gc.at[16 - n:16, h], shard - 2)
                if n < TILES:
                    act(1, red.at[n:TILES], gc.at[0:TILES - n, h], shard + 1)

    def passing_tile(n):
        u = TILES * w + n // XS
        q = n % XS
        src = red.at[n // XS, :, pl.ds(pl.multiple_of(q * LANE, LANE), LANE)]
        return src, mid.at[COLB * (5 * half + u // HALF) + x], 2 * q + h, HALF * h + u % HALF

    @pl.when(summing)
    def _():
        for n in range(XS - 1):
            arrived(xin.at[n], xr_sem.at[n])
        red[...] = (
            (part[x].astype(F32) + xin[0].astype(F32)) + (xin[1].astype(F32) + xin[2].astype(F32))
        ).astype(BF)
        to_homes(lambda n, src, dst, to: send(src, dst, gs_sem.at[n], gr_sem, rep, to).start())

        @pl.when(j == 1)
        def _():
            pltpu.make_async_copy(red, gc.at[pl.ds(TILES - r, TILES), h], gr_sem).start()

        def give_tile(n):
            src, dst, to_rep, to_shard = passing_tile(n)
            pass_on(src, dst, t1_sem.at[n], t1r_sem, to_rep, to_shard)

        loop(TILES * XS, give_tile)

    half_block = send(gc.at[:, h], gc.at[:, h], ge_sem.at[0], ge_sem.at[1], partner, shard)

    @pl.when(home)
    def _():
        arrived(gc.at[:, h], gr_sem)
        half_block.start()

    def view(hh, col):
        return g_own.at[:, :, hh, :, pl.ds(pl.multiple_of(col * LANE, LANE), LANE)]

    @pl.when(passing)
    def _():
        arrived(mid, t1r_sem)

        def give_slots(o):
            for n in range(2):
                outb[o, n] = mid[cell_of_slot[2 * o + n]]
            pass_on(outb.at[o], g_own.at[w, :, h, :, lanes], t2_sem.at[o], t2r_sem, rep, o)

        loop(SHARDS, give_slots)

    root = send(zb.at[h], zb.at[h], z_sem.at[0], z_sem.at[1], partner, shard)
    root_scale = send(scl.at[h], scl.at[h], z_sem.at[2], z_sem.at[3], partner, shard)

    def to_rows(act, n):
        act(0, pb.at[0:TILES - n, h], full.at[x, n:TILES, h], shard - 1)
        act(1, pb.at[10 - n:15 - n, h], full.at[x, :, h], shard + 1)
        act(2, pb.at[15 - n:16, h], full.at[x, 0:1 + n, h], shard + 2)

    @pl.when(home)
    def _():
        other = gc.at[:, 1 - h]
        arrived(other, ge_sem.at[1])
        g = gc[...].reshape(BLK, BLK)
        gt = g.T
        arrived(pv, p2r_sem)

        @pl.when(h == 0)
        def _():
            acc[...] = mm(g, gt)

        @pl.when(h == 1)
        def _():
            acc[...] = mm(gt, g)

        val = acc[...] + pv[...].reshape(BLK, BLK).astype(F32)
        scale = jnp.sum(jnp.where(eye(BLK), val, 0.0)) * (1.0 / BLK)
        zb[h] = root_less_one(val, scale)
        scl[h] = lax.rsqrt(jnp.sqrt(jnp.full((8, LANE), scale, F32)))
        root.start()
        root_scale.start()
        gf = g.astype(F32)
        sg = jnp.full((8, LANE), jnp.sum(gf * gf), F32)
        arrived(zb.at[1 - h], z_sem.at[1])
        arrived(scl.at[1 - h], z_sem.at[3])
        y = scl[0, 0:1, 0:1] * (gf + mm(zb[0], g))
        p = scl[1, 0:1, 0:1] * (y + mm(y.astype(BF), zb[1]))
        sp = jnp.full((8, LANE), jnp.sum(p * p), F32)
        ratio = jnp.sqrt(sg / (sp + 1e-06))[0:1, 0:1]
        pb[...] = (p * ratio).astype(BF).reshape(HALF, 2, SUB, BLK)
        for n in range(TILES):

            @pl.when(r == n)
            def _():
                to_rows(lambda i, src, dst, to: send(src, dst, ss_sem.at[i], sr_sem, rep, to).start(), n)
                pltpu.make_async_copy(pb.at[5 - n:10 - n, h], full.at[x, :, h], sr_sem).start()

    owned = view(h, x)
    arrived(owned, t2r_sem)
    outs = []
    for n in (2, 1, 3):
        outs.append(send(owned, owned, os_sem.at[n], or_sem.at[n], 2 * ((x + n) % XS) + h, shard))
    outs.append(send(owned, owned, os_sem.at[0], or_sem.at[0], partner, shard))
    for copy in outs:
        copy.start()

    rows = full.at[x, :, h]
    row_sends = [
        send(rows, rows, ds_sem.at[n], dr_sem.at[x], 2 * ((x + n) % XS) + h, shard) for n in (2, 1, 3)
    ]
    row_sends.append(send(rows, rows, ds_sem.at[0], dr_sem.at[COLB + x], partner, shard))

    @pl.when(summing)
    def _():
        arrived(rows, sr_sem)
        for copy in row_sends:
            copy.start()

    for n in (1, 3, 2):
        piece = view(h, (x + XS - n) % XS)
        arrived(piece, or_sem.at[n])
        copy = send(piece, piece, os_sem.at[3 + n], or_sem.at[3 + n], partner, shard)
        copy.start()
        outs.append(copy)

    def onward(c):
        return send(
            full.at[c, :, h], full.at[c, :, h], ds_sem.at[XS + c], dr_sem.at[COLB + c], partner, shard
        )

    for c in range(COLB):

        @pl.when(x != c)
        def _():
            arrived(full.at[c, :, h], dr_sem.at[c])
            onward(c).start()

    for c in range(COLB):
        arrived(full.at[c, :, 1 - h], dr_sem.at[COLB + c])
        d_out[:, :, :, c * BLK:(c + 1) * BLK] = full[c]
    for index, n in ((0, 0), (4, 1), (6, 3), (5, 2)):
        arrived(view(1 - h, (x + XS - n) % XS), or_sem.at[index])

    swap.wait_send()
    loop(SHARDS, lambda t: passed(pvb.at[t], p1_sem.at[t], p1r_sem, rep, t))

    def gave_factor(cell):
        to_rep, to_shard = home_of(cell)
        passed(po.at[cell], p2_sem.at[cell], p2r_sem, to_rep, to_shard)

    loop(CELLS, gave_factor)
    for c in range(COLB):

        @pl.when(x != c)
        def _():
            n = (c - x + XS) % XS - 1
            send(part.at[c], xin.at[n], xs_sem.at[c], xr_sem.at[n], 2 * c + h, shard).wait_send()
            onward(c).wait_send()

    @pl.when(summing)
    def _():
        to_homes(lambda n, src, dst, to: send(src, dst, gs_sem.at[n], gr_sem, rep, to).wait_send())

        def gave_tile(n):
            src, _, to_rep, to_shard = passing_tile(n)
            passed(src, t1_sem.at[n], t1r_sem, to_rep, to_shard)

        loop(TILES * XS, gave_tile)
        for copy in row_sends:
            copy.wait_send()

    @pl.when(passing)
    def _():
        loop(SHARDS, lambda o: passed(outb.at[o], t2_sem.at[o], t2r_sem, rep, o))

    @pl.when(home)
    def _():
        half_block.wait_send()
        root.wait_send()
        root_scale.wait_send()
        for n in range(TILES):

            @pl.when(r == n)
            def _():
                to_rows(lambda i, src, dst, to: send(src, dst, ss_sem.at[i], sr_sem, rep, to).wait_send(), n)

    for copy in outs:
        copy.wait_send()


def factors_kernel(live, g_in, left_prev, right_prev, left_new, right_new, lp, rp, ln, rn, in_sem, out_sem):
    shard = lax.axis_index("shard")
    loads = []
    for j in range(2):
        for src, dst, n in ((left_prev, lp, 0), (right_prev, rp, 1)):
            copy = pltpu.make_async_copy(src.at[j], dst.at[j], in_sem.at[2 * j + n])
            copy.start()
            loads.append(copy)
    stores = []
    for j in range(2):
        on = live[2 * shard + j] > 0
        g = g_in[:, j].reshape(BLK, BLK)
        g = jnp.where(on, g, jnp.zeros_like(g))
        gt = g.T
        for n, (prev, new, out, a, b) in enumerate(
            ((lp, ln, left_new, g, gt), (rp, rn, right_new, gt, g))
        ):
            prod = mm(a, b)
            loads[2 * j + n].wait()
            new[j] = jnp.where(on, prev[j] + prod, 0.0)
            copy = pltpu.make_async_copy(new.at[j], out.at[j], out_sem.at[2 * j + n])
            copy.start()
            stores.append(copy)
    for copy in stores:
        copy.wait()


def tables(block_owner, block_row, block_col):
    count = block_owner.shape[0]
    index = jnp.arange(count, dtype=jnp.int32)
    earlier = (block_owner[:, None] == block_owner[None, :]) & (index[None, :] < index[:, None])
    slot = 2 * block_owner + jnp.sum(earlier.astype(jnp.int32), axis=1)
    cell = block_row // BLK * COLB + block_col // BLK
    at_slot = (slot[None, :] == jnp.arange(2 * SHARDS, dtype=jnp.int32)[:, None]).astype(jnp.int32)
    at_cell = (cell[None, :] == jnp.arange(CELLS, dtype=jnp.int32)[:, None]).astype(jnp.int32)
    cell_of_slot = jnp.sum(at_slot * cell[None, :], axis=1)
    live = jnp.sum(at_slot, axis=1)
    slot_of_cell = jnp.sum(at_cell * slot[None, :], axis=1)
    return cell_of_slot, live, slot_of_cell


SMEM = pl.BlockSpec(memory_space=pltpu.SMEM)
VMEM = pl.BlockSpec(memory_space=pltpu.VMEM)
ANY = pl.BlockSpec(memory_space=pl.ANY)
DMA = pltpu.SemaphoreType.DMA


def body(grads, left_prev, right_prev, block_owner, block_row, block_col):
    cell_of_slot, live, slot_of_cell = tables(block_owner, block_row, block_col)
    rows = grads.shape[1]
    direction, gathered = pl.pallas_call(
        step_kernel,
        out_shape=(
            jax.ShapeDtypeStruct((TILES, 2, SUB, COLB * BLK), BF),
            jax.ShapeDtypeStruct((HALF, 2, 2, SUB, BLK), BF),
        ),
        in_specs=[SMEM, SMEM, ANY, ANY, ANY],
        out_specs=(VMEM, VMEM),
        scratch_shapes=[
            pltpu.VMEM((TILES, SUB, COLB * BLK), BF),
            pltpu.VMEM((TILES, SUB, COLB * BLK), BF),
            pltpu.VMEM((COLB, TILES, SUB, BLK), BF),
            pltpu.VMEM((XS - 1, TILES, SUB, BLK), BF),
            pltpu.VMEM((TILES, SUB, BLK), BF),
            pltpu.VMEM((2, 2 * HALF, SUB, LANE), F32),
            pltpu.VMEM((2 * HALF, 2, SUB, LANE), BF),
            pltpu.VMEM((2 * SHARDS, SUB, LANE), BF),
            pltpu.VMEM((CELLS, SUB, LANE), BF),
            pltpu.VMEM((2 * HALF, SUB, BLK), BF),
            pltpu.VMEM((HALF, 2, SUB, BLK), BF),
            pltpu.VMEM((CELLS, SUB, LANE), BF),
            pltpu.VMEM((SHARDS, 2, SUB, LANE), BF),
            pltpu.VMEM((BLK, BLK), F32),
            pltpu.VMEM((2, BLK, BLK), BF),
            pltpu.VMEM((2, 8, LANE), F32),
            pltpu.VMEM((HALF, 2, SUB, BLK), BF),
            pltpu.VMEM((COLB, TILES, 2, SUB, BLK), BF),
            DMA, DMA, DMA((2,)), DMA((3,)), DMA((3,)),
            DMA((SHARDS,)), DMA, DMA((CELLS,)), DMA, DMA((2,)), DMA, DMA((2,)),
            DMA((TILES * XS,)), DMA, DMA((SHARDS,)), DMA, DMA((7,)), DMA((7,)),
            DMA((4,)), DMA((3,)), DMA, DMA((7,)), DMA((6,)), pltpu.SemaphoreType.REGULAR,
        ],
        compiler_params=pltpu.CompilerParams(
            collective_id=0, has_side_effects=True, vmem_limit_bytes=58 * 1024 * 1024
        ),
        name="shampoo_step",
    )(
        cell_of_slot,
        slot_of_cell,
        grads.reshape(TILES, 2, SUB, COLB * BLK),
        left_prev.reshape(2, 2 * HALF, SUB, BLK),
        right_prev.reshape(2, 2 * HALF, SUB, BLK),
    )

    sq = jax.ShapeDtypeStruct((2, BLK, BLK), F32)
    left_new, right_new = pl.pallas_call(
        factors_kernel,
        out_shape=(sq, sq),
        in_specs=[SMEM, VMEM, ANY, ANY],
        out_specs=(ANY, ANY),
        scratch_shapes=[pltpu.VMEM((2, BLK, BLK), F32)] * 4 + [DMA((4,)), DMA((4,))],
        compiler_params=pltpu.CompilerParams(vmem_limit_bytes=58 * 1024 * 1024),
        cost_estimate=pl.CostEstimate(flops=4 * 2 * BLK**3, bytes_accessed=8 * 2**20, transcendentals=0),
        name="new_factors",
    )(live, gathered, left_prev, right_prev)
    return direction.reshape(rows, COLB * BLK), left_new, right_new


def solution(mesh):
    in_specs = (P("rep", "shard", None), P("shard", None, None), P("shard", None, None), P(), P(), P())
    out_specs = (P("shard", None), P("shard", None, None), P("shard", None, None))
    return jax.shard_map(body, mesh=mesh, in_specs=in_specs, out_specs=out_specs, check_vma=False)
```

time: 80.6 us -> 63.5 us (0.79)
  the two profiles are of different devices: /device:TPU:1 before, /device:TPU:43 now
where the time goes in v3:
time: 63.5 us; the launch traced here: 63.3 us
  Pallas kernels  59 us (93%)
  other arithmetic  2.84 us (4%)
  local copies, waits for them, and re-layouts  0.79 us (1%)
  between operations  0.66 us (1%)
    pallas_call x1, Pallas kernels, body(): pl.pallas_call(step_kernel, out_shape=(jax.ShapeDtypeStruct((TILES, 2, SU...  53.5 us
    pallas_call x1, Pallas kernels, body(): pl.pallas_call(factors_kernel, out_shape=(sq, sq), in_specs=[SMEM, VMEM,...  5.59 us

profile of v3, /device:TPU:43, one launch (start us, length us, event | category | flops | bytes accessed | tf_op | source)
XLA Modules:
  0.0 63.3 jit_solution(9806953035374414378)
XLA Ops:
  0.6 0.9 %convert_reduce_fusion.1 = s32[30]{0:T(128)S(1)} fusion(s32[30]{0:T(128)} %param.9), kind=kLoop, calls=%fused_computation.5 | loop fusion | flops 4470 | bytes 240 | tf_op jit(solution)/shard_map/reduce_sum | solution.py:403
  1.5 0.7 %fusion.1 = (s32[30]{0:T(128)S(1)}, s32[30]{0:T(128)S(1)}) fusion(s32[30]{0:T(128)} %param.11, s32[30]{0:T(128)} %param.10, s32[30]{0:T(128)S(1)} %convert_reduce_fusion.1, s32[30]{0:T(128)} %param.9), kind=kLoop, calls=%fused_computation.16 | loop fusion | flops 1020 | bytes 720 | tf_op jit(solution)/shard_map/add | solution.py:404
  2.2 0.6 select_reduce_fusion.slot_of_cell
  2.9 0.6 convert_reduce_fusion
  3.5 53.5 %shampoo_step.1 = (bf16[5,2,16,1536]{3,2,1,0:T(8,128)(2,1)}, bf16[16,2,2,16,512]{4,3,2,1,0:T(8,128)(2,1)}) custom-call(s32[64]{0:T(128)} %get-tuple-element.12.cell_of_slot, s32[30]{0:T(128)} %select_reduce_fusion.slot_of_cell, bf16[5,2,16,1536]{3,2,1,0:T(8,128)(2,1)} %bitcast.6, f32[2,32,16,512]{3,2,1,0:T(8,128)} %bitcast.4, f32[2,32,16,512]{3,2,1,0:T(8,128)} %bitcast.5), custom_call_target="tpu_custom_call" | custom-call | tf_op jit(solution)/shard_map/shampoo_step/pallas_call | solution.py:422
  56.9 0.0 copy-start
  57.0 5.6 %new_factors.1 = (f32[2,512,512]{2,1,0:T(8,128)}, f32[2,512,512]{2,1,0:T(8,128)}) custom-call(s32[64]{0:T(128)} %get-tuple-element.11.live, bf16[16,2,2,16,512]{4,3,2,1,0:T(8,128)(2,1)} %get-tuple-element.8.g_in, f32[2,512,512]{2,1,0:T(8,128)} %left_prev.1, f32[2,512,512]{2,1,0:T(8,128)} %right_prev.1), custom_call_target="tpu_custom_call" | custom-call | flops 1073741824 | bytes 8388608 | tf_op jit(solution)/shard_map/new_factors/pallas_call | solution.py:467
  62.5 0.0 copy-done
  62.6 0.8 %copy.10 = bf16[160,1536]{1,0:T(8,128)(2,1)} copy(bf16[160,1536]{1,0:T(8,128)(2,1)S(1)} %bitcast.7) | data formatting | bytes 983040
Async XLA Ops:
  56.9 5.6 %copy-start = (bf16[5,2,16,1536]{3,2,1,0:T(8,128)(2,1)S(1)}, bf16[5,2,16,1536]{3,2,1,0:T(8,128)(2,1)}, u32[]{:S(2)}) copy-start(bf16[5,2,16,1536]{3,2,1,0:T(8,128)(2,1)} %get-tuple-element.7) | copy-start | bytes 1474564

commit v4 on v3

--- a/solution.py
+++ b/solution.py
@@ -65,11 +65,29 @@
     return z.astype(BF)
 
 
+def fill_tables(tab, block_owner, block_row, block_col):
+    sub = lax.broadcasted_iota(jnp.int32, (32, LANE), 0)
+    lane = lax.broadcasted_iota(jnp.int32, (32, LANE), 1)
+    owner = jnp.full((32, LANE), -1, jnp.int32)
+    other = jnp.full((32, LANE), -2, jnp.int32)
+    cell = jnp.full((32, LANE), -1, jnp.int32)
+    for b in range(CELLS):
+        owner = jnp.where(sub == b, block_owner[b], owner)
+        other = jnp.where(lane == b, block_owner[b], other)
+        cell = jnp.where(sub == b, block_row[b] // BLK * COLB + block_col[b] // BLK, cell)
+    earlier = ((owner == other) & (lane < sub)).astype(jnp.int32)
+    slot = 2 * owner + jnp.sum(earlier, axis=1, keepdims=True)
+    cells = jnp.sum(jnp.where(slot == lane, cell, 0), axis=0, keepdims=True)
+    slots = jnp.sum(jnp.where(cell == lane, slot, 0), axis=0, keepdims=True)
+    tab[0:1] = jnp.clip(cells, 0, CELLS - 1)
+    tab[1:2] = jnp.clip(slots, 0, 2 * SHARDS - 1)
+
+
 def step_kernel(
-    cell_of_slot, slot_of_cell, grads, left_prev, right_prev, d_out, g_own,
-    own, pair, part, xin, red, pvf, pvb, pm, po, pv, gc, mid, outb, acc, zb, scl, pb, full,
+    block_owner, block_row, block_col, grads, left_prev, right_prev, d_out, g_out,
+    g_own, own, pair, part, xin, red, pvf, pvb, pm, po, pv, gc, mid, outb, acc, zb, scl, pb, full, tab, look,
     own_sem, pvf_sem, pair_sem, xs_sem, xr_sem, p1_sem, p1r_sem, p2_sem, p2r_sem, gs_sem, gr_sem, ge_sem,
-    t1_sem, t1r_sem, t2_sem, t2r_sem, os_sem, or_sem, z_sem, ss_sem, sr_sem, ds_sem, dr_sem, ready,
+    t1_sem, t1r_sem, t2_sem, t2r_sem, os_sem, or_sem, z_sem, ss_sem, sr_sem, ds_sem, dr_sem, tab_sem, out_sem, ready,
 ):
     rep = lax.axis_index("rep")
     shard = lax.axis_index("shard")
@@ -97,13 +115,6 @@
         def _():
             pltpu.make_async_copy(src, dst, recv_sem).start()
 
-    def passed(src, send_sem, recv_sem, to_rep, to_shard):
-        me = (to_rep == rep) & (to_shard == shard)
-
-        @pl.when(jnp.logical_not(me))
-        def _():
-            send(src, src, send_sem, recv_sem, to_rep, to_shard).wait_send()
-
     def arrived(ref, sem):
         pltpu.make_async_copy(ref, ref, sem).wait()
 
@@ -129,11 +140,15 @@
     for n in range(1, XS):
         greet(barrier, 2 * ((x + n) % XS) + h, shard)
     greet(barrier, partner, shard)
+    fill_tables(tab, block_owner, block_row, block_col)
+    tables = pltpu.make_async_copy(tab, look, tab_sem)
+    tables.start()
     arrived(pvf, pvf_sem)
     for n in range(2):
         pvb[:, n] = pvf[n].astype(BF)
     pl.semaphore_wait(barrier, SHARDS - 1 + XS)
 
+    tables.wait()
     swap = send(grads.at[:, 1 - h], pair, pair_sem.at[0], pair_sem.at[1], partner, shard)
     swap.start()
     for n in range(1, XS):
@@ -141,7 +156,12 @@
             ready, inc=1, device_id=(2 * ((x + n) % XS) + h, shard), device_id_type=MESH
         )
     mine = pm.at[pl.ds(2 * shard, 2)]
-    loop(SHARDS, lambda t: pass_on(pvb.at[t], mine, p1_sem.at[t], p1r_sem, rep, t))
+    def give_old(n):
+        t = (shard + 1 + n) % SHARDS
+        send(pvb.at[t], mine, p1_sem, p1r_sem, rep, t).start()
+
+    loop(SHARDS - 1, give_old)
+    pltpu.make_async_copy(pvb.at[shard], mine, p1r_sem).start()
 
     load.wait()
     swap.wait_recv()
@@ -163,12 +183,22 @@
         row = cell // COLB
         return 2 * (cell % COLB) + h, HALF * (row // 5) + 3 * (row % 5) + 1
 
-    def give_factor(cell):
-        po[cell] = pm[slot_of_cell[cell]]
+    own_cell = COLB * (5 * half + r) + x
+    first = jnp.where(home, own_cell + 1, 0)
+
+    def give_factor(n):
+        cell = (first + n) % CELLS
+        po[cell] = pm[look[1, cell]]
         to_rep, to_shard = home_of(cell)
-        pass_on(po.at[cell], tile_at_home, p2_sem.at[cell], p2r_sem, to_rep, to_shard)
-
-    loop(CELLS, give_factor)
+        send(po.at[cell], tile_at_home, p2_sem, p2r_sem, to_rep, to_shard).start()
+
+    loop(CELLS - home.astype(jnp.int32), give_factor)
+
+    @pl.when(home)
+    def _():
+        po[own_cell] = pm[look[1, own_cell]]
+        pltpu.make_async_copy(po.at[own_cell], tile_at_home, p2r_sem).start()
+
 
     def to_homes(act):
         @pl.when(j == 2)
@@ -205,7 +235,7 @@
 
         def give_tile(n):
             src, dst, to_rep, to_shard = passing_tile(n)
-            pass_on(src, dst, t1_sem.at[n], t1r_sem, to_rep, to_shard)
+            pass_on(src, dst, t1_sem, t1r_sem, to_rep, to_shard)
 
         loop(TILES * XS, give_tile)
 
@@ -223,12 +253,20 @@
     def _():
         arrived(mid, t1r_sem)
 
-        def give_slots(o):
+        def fill(o):
             for n in range(2):
-                outb[o, n] = mid[cell_of_slot[2 * o + n]]
-            pass_on(outb.at[o], g_own.at[w, :, h, :, lanes], t2_sem.at[o], t2r_sem, rep, o)
-
-        loop(SHARDS, give_slots)
+                outb[o, n] = mid[look[0, 2 * o + n]]
+
+        slots_at_owner = g_own.at[w, :, h, :, lanes]
+
+        def give_slots(n):
+            o = (shard + 1 + n) % SHARDS
+            fill(o)
+            send(outb.at[o], slots_at_owner, t2_sem, t2r_sem, rep, o).start()
+
+        loop(SHARDS - 1, give_slots)
+        fill(shard)
+        pltpu.make_async_copy(outb.at[shard], slots_at_owner, t2r_sem).start()
 
     root = send(zb.at[h], zb.at[h], z_sem.at[0], z_sem.at[1], partner, shard)
     root_scale = send(scl.at[h], scl.at[h], z_sem.at[2], z_sem.at[3], partner, shard)
@@ -316,20 +354,28 @@
             arrived(full.at[c, :, h], dr_sem.at[c])
             onward(c).start()
 
+    for index, n in ((0, 0), (4, 1), (6, 3), (5, 2)):
+        arrived(view(1 - h, (x + XS - n) % XS), or_sem.at[index])
+    g_store = pltpu.make_async_copy(g_own, g_out, out_sem.at[COLB])
+    g_store.start()
+    d_stores = []
     for c in range(COLB):
         arrived(full.at[c, :, 1 - h], dr_sem.at[COLB + c])
-        d_out[:, :, :, c * BLK:(c + 1) * BLK] = full[c]
-    for index, n in ((0, 0), (4, 1), (6, 3), (5, 2)):
-        arrived(view(1 - h, (x + XS - n) % XS), or_sem.at[index])
+        copy = pltpu.make_async_copy(full.at[c], d_out.at[:, :, :, pl.ds(c * BLK, BLK)], out_sem.at[c])
+        copy.start()
+        d_stores.append(copy)
 
     swap.wait_send()
-    loop(SHARDS, lambda t: passed(pvb.at[t], p1_sem.at[t], p1r_sem, rep, t))
-
-    def gave_factor(cell):
-        to_rep, to_shard = home_of(cell)
-        passed(po.at[cell], p2_sem.at[cell], p2r_sem, to_rep, to_shard)
-
-    loop(CELLS, gave_factor)
+    arrived(pvb.at[0:SHARDS - 1], p1_sem)
+
+    @pl.when(home)
+    def _():
+        arrived(po.at[0:CELLS - 1], p2_sem)
+
+    @pl.when(jnp.logical_not(home))
+    def _():
+        arrived(po, p2_sem)
+
     for c in range(COLB):
 
         @pl.when(x != c)
@@ -342,17 +388,22 @@
     def _():
         to_homes(lambda n, src, dst, to: send(src, dst, gs_sem.at[n], gr_sem, rep, to).wait_send())
 
-        def gave_tile(n):
-            src, _, to_rep, to_shard = passing_tile(n)
-            passed(src, t1_sem.at[n], t1r_sem, to_rep, to_shard)
-
-        loop(TILES * XS, gave_tile)
+        kept = passing & ((12 * w) % HALF < TILES)
+
+        @pl.when(kept)
+        def _():
+            arrived(mid.at[0:TILES * XS - 1], t1_sem)
+
+        @pl.when(jnp.logical_not(kept))
+        def _():
+            arrived(mid.at[0:TILES * XS], t1_sem)
+
         for copy in row_sends:
             copy.wait_send()
 
     @pl.when(passing)
     def _():
-        loop(SHARDS, lambda o: passed(outb.at[o], t2_sem.at[o], t2r_sem, rep, o))
+        arrived(outb.at[0:SHARDS - 1], t2_sem)
 
     @pl.when(home)
     def _():
@@ -367,47 +418,48 @@
 
     for copy in outs:
         copy.wait_send()
-
-
-def factors_kernel(live, g_in, left_prev, right_prev, left_new, right_new, lp, rp, ln, rn, in_sem, out_sem):
+    g_store.wait()
+    for copy in d_stores:
+        copy.wait()
+
+
+def finish_kernel(block_owner, d_in, g_in, left_prev, right_prev, d_out, left_new, right_new,
+                  db, gb, lp, rp, ln, rn, d_sem, in_sem, out_sem):
     shard = lax.axis_index("shard")
     loads = []
     for j in range(2):
-        for src, dst, n in ((left_prev, lp, 0), (right_prev, rp, 1)):
-            copy = pltpu.make_async_copy(src.at[j], dst.at[j], in_sem.at[2 * j + n])
+        for src, dst, n in ((g_in, gb, 2), (left_prev, lp, 0), (right_prev, rp, 1)):
+            if n == 2:
+                copy = pltpu.make_async_copy(src.at[:, j], dst.at[:, j], in_sem.at[3 * j + n])
+            else:
+                copy = pltpu.make_async_copy(src.at[j], dst.at[j], in_sem.at[3 * j + n])
             copy.start()
             loads.append(copy)
+    d_load = pltpu.make_async_copy(d_in, db, d_sem.at[0])
+    d_load.start()
+    held = lax.fori_loop(0, CELLS, lambda b, n: n + (block_owner[b] == shard).astype(jnp.int32), 0)
     stores = []
     for j in range(2):
-        on = live[2 * shard + j] > 0
-        g = g_in[:, j].reshape(BLK, BLK)
+        on = held > j
+        loads[3 * j].wait()
+        g = gb[:, j].reshape(BLK, BLK)
         g = jnp.where(on, g, jnp.zeros_like(g))
         gt = g.T
         for n, (prev, new, out, a, b) in enumerate(
             ((lp, ln, left_new, g, gt), (rp, rn, right_new, gt, g))
         ):
             prod = mm(a, b)
-            loads[2 * j + n].wait()
+            loads[3 * j + 1 + n].wait()
             new[j] = jnp.where(on, prev[j] + prod, 0.0)
             copy = pltpu.make_async_copy(new.at[j], out.at[j], out_sem.at[2 * j + n])
             copy.start()
             stores.append(copy)
+    d_load.wait()
+    d_store = pltpu.make_async_copy(db, d_out, d_sem.at[1])
+    d_store.start()
+    d_store.wait()
     for copy in stores:
         copy.wait()
-
-
-def tables(block_owner, block_row, block_col):
-    count = block_owner.shape[0]
-    index = jnp.arange(count, dtype=jnp.int32)
-    earlier = (block_owner[:, None] == block_owner[None, :]) & (index[None, :] < index[:, None])
-    slot = 2 * block_owner + jnp.sum(earlier.astype(jnp.int32), axis=1)
-    cell = block_row // BLK * COLB + block_col // BLK
-    at_slot = (slot[None, :] == jnp.arange(2 * SHARDS, dtype=jnp.int32)[:, None]).astype(jnp.int32)
-    at_cell = (cell[None, :] == jnp.arange(CELLS, dtype=jnp.int32)[:, None]).astype(jnp.int32)
-    cell_of_slot = jnp.sum(at_slot * cell[None, :], axis=1)
-    live = jnp.sum(at_slot, axis=1)
-    slot_of_cell = jnp.sum(at_cell * slot[None, :], axis=1)
-    return cell_of_slot, live, slot_of_cell
 
 
 SMEM = pl.BlockSpec(memory_space=pltpu.SMEM)
@@ -417,7 +469,6 @@
 
 
 def body(grads, left_prev, right_prev, block_owner, block_row, block_col):
-    cell_of_slot, live, slot_of_cell = tables(block_owner, block_row, block_col)
     rows = grads.shape[1]
     direction, gathered = pl.pallas_call(
         step_kernel,
@@ -425,9 +476,10 @@
             jax.ShapeDtypeStruct((TILES, 2, SUB, COLB * BLK), BF),
             jax.ShapeDtypeStruct((HALF, 2, 2, SUB, BLK), BF),
         ),
-        in_specs=[SMEM, SMEM, ANY, ANY, ANY],
-        out_specs=(VMEM, VMEM),
+        in_specs=[SMEM, SMEM, SMEM, ANY, ANY, ANY],
+        out_specs=(ANY, ANY),
         scratch_shapes=[
+            pltpu.VMEM((HALF, 2, 2, SUB, BLK), BF),
             pltpu.VMEM((TILES, SUB, COLB * BLK), BF),
             pltpu.VMEM((TILES, SUB, COLB * BLK), BF),
             pltpu.VMEM((COLB, TILES, SUB, BLK), BF),
@@ -446,34 +498,42 @@
             pltpu.VMEM((2, 8, LANE), F32),
             pltpu.VMEM((HALF, 2, SUB, BLK), BF),
             pltpu.VMEM((COLB, TILES, 2, SUB, BLK), BF),
+            pltpu.VMEM((8, LANE), jnp.int32),
+            pltpu.SMEM((8, LANE), jnp.int32),
             DMA, DMA, DMA((2,)), DMA((3,)), DMA((3,)),
-            DMA((SHARDS,)), DMA, DMA((CELLS,)), DMA, DMA((2,)), DMA, DMA((2,)),
-            DMA((TILES * XS,)), DMA, DMA((SHARDS,)), DMA, DMA((7,)), DMA((7,)),
-            DMA((4,)), DMA((3,)), DMA, DMA((7,)), DMA((6,)), pltpu.SemaphoreType.REGULAR,
+            DMA, DMA, DMA, DMA, DMA((2,)), DMA, DMA((2,)), DMA, DMA, DMA, DMA, DMA((7,)), DMA((7,)),
+            DMA((4,)), DMA((3,)), DMA, DMA((7,)), DMA((6,)), DMA, DMA((4,)), pltpu.SemaphoreType.REGULAR,
         ],
         compiler_params=pltpu.CompilerParams(
             collective_id=0, has_side_effects=True, vmem_limit_bytes=58 * 1024 * 1024
         ),
         name="shampoo_step",
     )(
-        cell_of_slot,
-        slot_of_cell,
+        block_owner,
+        block_row,
+        block_col,
         grads.reshape(TILES, 2, SUB, COLB * BLK),
         left_prev.reshape(2, 2 * HALF, SUB, BLK),
         right_prev.reshape(2, 2 * HALF, SUB, BLK),
     )
 
+    rows_t = jax.ShapeDtypeStruct((TILES, 2, SUB, COLB * BLK), BF)
     sq = jax.ShapeDtypeStruct((2, BLK, BLK), F32)
-    left_new, right_new = pl.pallas_call(
-        factors_kernel,
-        out_shape=(sq, sq),
-        in_specs=[SMEM, VMEM, ANY, ANY],
-        out_specs=(ANY, ANY),
-        scratch_shapes=[pltpu.VMEM((2, BLK, BLK), F32)] * 4 + [DMA((4,)), DMA((4,))],
+    direction, left_new, right_new = pl.pallas_call(
+        finish_kernel,
+        out_shape=(rows_t, sq, sq),
+        in_specs=[SMEM, ANY, ANY, ANY, ANY],
+        out_specs=(ANY, ANY, ANY),
+        scratch_shapes=[
+            pltpu.VMEM((TILES, 2, SUB, COLB * BLK), BF),
+            pltpu.VMEM((HALF, 2, 2, SUB, BLK), BF),
+        ]
+        + [pltpu.VMEM((2, BLK, BLK), F32)] * 4
+        + [DMA((2,)), DMA((6,)), DMA((4,))],
         compiler_params=pltpu.CompilerParams(vmem_limit_bytes=58 * 1024 * 1024),
-        cost_estimate=pl.CostEstimate(flops=4 * 2 * BLK**3, bytes_accessed=8 * 2**20, transcendentals=0),
+        cost_estimate=pl.CostEstimate(flops=4 * 2 * BLK**3, bytes_accessed=10 * 2**20, transcendentals=0),
         name="new_factors",
-    )(live, gathered, left_prev, right_prev)
+    )(block_owner, direction, gathered, left_prev, right_prev)
     return direction.reshape(rows, COLB * BLK), left_new, right_new
 
 

time: 63.5 us -> 57.8 us (0.910)
  the two profiles are of different devices: /device:TPU:43 before, /device:TPU:1 now
where the time goes in v4:
time: 57.8 us; the launch traced here: 57.7 us
  Pallas kernels  57.1 us (99%)
  between operations  0.64 us (1%)
    pallas_call x1, Pallas kernels, body(): pl.pallas_call(step_kernel, out_shape=(jax.ShapeDtypeStruct((TILES, 2, SU...  51.6 us
    pallas_call x1, Pallas kernels, body(): pl.pallas_call(finish_kernel, out_shape=(rows_t, sq, sq), in_specs=[SMEM,...  5.5 us

profile of v4, /device:TPU:1, one launch (start us, length us, event | category | flops | bytes accessed | tf_op | source)
XLA Modules:
  0.0 57.7 jit_solution(343830673278897536)
XLA Ops:
  0.6 51.6 %shampoo_step.1 = (bf16[5,2,16,1536]{3,2,1,0:T(8,128)(2,1)}, bf16[16,2,2,16,512]{4,3,2,1,0:T(8,128)(2,1)}) custom-call(s32[30]{0:T(128)} %block_owner.3, s32[30]{0:T(128)} %block_row.1, s32[30]{0:T(128)} %block_col.1, bf16[5,2,16,1536]{3,2,1,0:T(8,128)(2,1)} %bitcast.6, f32[2,32,16,512]{3,2,1,0:T(8,128)} %bitcast.4, f32[2,32,16,512]{3,2,1,0:T(8,128)} %bitcast.5), custom_call_target="tpu_custom_call" | custom-call | tf_op jit(solution)/shard_map/shampoo_step/pallas_call | solution.py:473
  52.2 5.5 %new_factors.1 = (bf16[5,2,16,1536]{3,2,1,0:T(8,128)(2,1)}, f32[2,512,512]{2,1,0:T(8,128)}, f32[2,512,512]{2,1,0:T(8,128)}) custom-call(s32[30]{0:T(128)} %block_owner.3, bf16[5,2,16,1536]{3,2,1,0:T(8,128)(2,1)} %get-tuple-element.8.d_in, bf16[16,2,2,16,512]{4,3,2,1,0:T(8,128)(2,1)} %get-tuple-element.9.g_in, f32[2,512,512]{2,1,0:T(8,128)} %left_prev.1, ...), custom_call_target="tpu_custom_call" | custom-call | flops 1073741824 | bytes 10485760 | tf_op jit(solution)/shard_map/new_factors/pallas_call | solution.py:522

commit v5 on v4

--- a/solution.py
+++ b/solution.py
@@ -81,13 +81,14 @@
     slots = jnp.sum(jnp.where(cell == lane, slot, 0), axis=0, keepdims=True)
     tab[0:1] = jnp.clip(cells, 0, CELLS - 1)
     tab[1:2] = jnp.clip(slots, 0, 2 * SHARDS - 1)
+    tab[2:3] = jnp.sum((slot == lane).astype(jnp.int32), axis=0, keepdims=True)
 
 
 def step_kernel(
-    block_owner, block_row, block_col, grads, left_prev, right_prev, d_out, g_out,
-    g_own, own, pair, part, xin, red, pvf, pvb, pm, po, pv, gc, mid, outb, acc, zb, scl, pb, full, tab, look,
+    block_owner, block_row, block_col, grads, left_prev, right_prev, d_out, left_out, right_out,
+    g_own, lp, rp, own, pair, part, xin, red, pvf, pvb, pm, po, pv, gc, mid, outb, acc, zb, scl, pb, full, tab, look,
     own_sem, pvf_sem, pair_sem, xs_sem, xr_sem, p1_sem, p1r_sem, p2_sem, p2r_sem, gs_sem, gr_sem, ge_sem,
-    t1_sem, t1r_sem, t2_sem, t2r_sem, os_sem, or_sem, z_sem, ss_sem, sr_sem, ds_sem, dr_sem, tab_sem, out_sem, ready,
+    t1_sem, t1r_sem, t2_sem, t2r_sem, os_sem, or_sem, z_sem, ss_sem, sr_sem, ds_sem, dr_sem, tab_sem, in_sem, ready,
 ):
     rep = lax.axis_index("rep")
     shard = lax.axis_index("shard")
@@ -136,6 +137,12 @@
     def _():
         pltpu.make_async_copy(right_prev.at[:, :, :, lanes], pvf, pvf_sem).start()
 
+    whole = [
+        pltpu.make_async_copy(left_prev, lp, in_sem.at[0]),
+        pltpu.make_async_copy(right_prev, rp, in_sem.at[1]),
+    ]
+    for copy in whole:
+        copy.start()
     loop(SHARDS - 1, lambda n: greet(barrier, rep, (shard + 1 + n) % SHARDS))
     for n in range(1, XS):
         greet(barrier, 2 * ((x + n) % XS) + h, shard)
@@ -356,14 +363,22 @@
 
     for index, n in ((0, 0), (4, 1), (6, 3), (5, 2)):
         arrived(view(1 - h, (x + XS - n) % XS), or_sem.at[index])
-    g_store = pltpu.make_async_copy(g_own, g_out, out_sem.at[COLB])
-    g_store.start()
-    d_stores = []
+    for copy in whole:
+        copy.wait()
+
+    def factors(n):
+        on = look[2, 2 * shard + n] > 0
+        g = g_own[:, n].reshape(BLK, BLK)
+        g = jnp.where(on, g, jnp.zeros_like(g))
+        gt = g.T
+        for prev, out, a, b in ((lp, left_out, g, gt), (rp, right_out, gt, g)):
+            new = prev[n].reshape(BLK, BLK) + mm(a, b)
+            out[n] = jnp.where(on, new, jnp.zeros_like(new))
+
+    loop(2, factors)
     for c in range(COLB):
         arrived(full.at[c, :, 1 - h], dr_sem.at[COLB + c])
-        copy = pltpu.make_async_copy(full.at[c], d_out.at[:, :, :, pl.ds(c * BLK, BLK)], out_sem.at[c])
-        copy.start()
-        d_stores.append(copy)
+        d_out[:, :, :, c * BLK:(c + 1) * BLK] = full[c]
 
     swap.wait_send()
     arrived(pvb.at[0:SHARDS - 1], p1_sem)
@@ -418,47 +433,17 @@
 
     for copy in outs:
         copy.wait_send()
-    g_store.wait()
-    for copy in d_stores:
-        copy.wait()
-
-
-def finish_kernel(block_owner, d_in, g_in, left_prev, right_prev, d_out, left_new, right_new,
-                  db, gb, lp, rp, ln, rn, d_sem, in_sem, out_sem):
-    shard = lax.axis_index("shard")
-    loads = []
-    for j in range(2):
-        for src, dst, n in ((g_in, gb, 2), (left_prev, lp, 0), (right_prev, rp, 1)):
-            if n == 2:
-                copy = pltpu.make_async_copy(src.at[:, j], dst.at[:, j], in_sem.at[3 * j + n])
-            else:
-                copy = pltpu.make_async_copy(src.at[j], dst.at[j], in_sem.at[3 * j + n])
-            copy.start()
-            loads.append(copy)
-    d_load = pltpu.make_async_copy(d_in, db, d_sem.at[0])
-    d_load.start()
-    held = lax.fori_loop(0, CELLS, lambda b, n: n + (block_owner[b] == shard).astype(jnp.int32), 0)
-    stores = []
-    for j in range(2):
-        on = held > j
-        loads[3 * j].wait()
-        g = gb[:, j].reshape(BLK, BLK)
-        g = jnp.where(on, g, jnp.zeros_like(g))
-        gt = g.T
-        for n, (prev, new, out, a, b) in enumerate(
-            ((lp, ln, left_new, g, gt), (rp, rn, right_new, gt, g))
-        ):
-            prod = mm(a, b)
-            loads[3 * j + 1 + n].wait()
-            new[j] = jnp.where(on, prev[j] + prod, 0.0)
-            copy = pltpu.make_async_copy(new.at[j], out.at[j], out_sem.at[2 * j + n])
-            copy.start()
-            stores.append(copy)
-    d_load.wait()
-    d_store = pltpu.make_async_copy(db, d_out, d_sem.at[1])
-    d_store.start()
-    d_store.wait()
-    for copy in stores:
+
+
+def store_kernel(d_in, left_in, right_in, d_out, left_new, right_new, sem):
+    copies = []
+    for n, (src, dst) in enumerate(((left_in, left_new), (right_in, right_new))):
+        for j in range(2):
+            copies.append(pltpu.make_async_copy(src.at[j], dst.at[j], sem.at[2 * n + j]))
+    copies.append(pltpu.make_async_copy(d_in, d_out, sem.at[4]))
+    for copy in copies:
+        copy.start()
+    for copy in copies:
         copy.wait()
 
 
@@ -470,16 +455,19 @@
 
 def body(grads, left_prev, right_prev, block_owner, block_row, block_col):
     rows = grads.shape[1]
-    direction, gathered = pl.pallas_call(
+    direction, left_new, right_new = pl.pallas_call(
         step_kernel,
         out_shape=(
-            jax.ShapeDtypeStruct((TILES, 2, SUB, COLB * BLK), BF),
-            jax.ShapeDtypeStruct((HALF, 2, 2, SUB, BLK), BF),
+            pltpu.VMEM((TILES, 2, SUB, COLB * BLK), BF),
+            pltpu.VMEM((2, BLK, BLK), F32),
+            pltpu.VMEM((2, BLK, BLK), F32),
         ),
         in_specs=[SMEM, SMEM, SMEM, ANY, ANY, ANY],
-        out_specs=(ANY, ANY),
+        out_specs=(VMEM, VMEM, VMEM),
         scratch_shapes=[
             pltpu.VMEM((HALF, 2, 2, SUB, BLK), BF),
+            pltpu.VMEM((2, 2 * HALF, SUB, BLK), F32),
+            pltpu.VMEM((2, 2 * HALF, SUB, BLK), F32),
             pltpu.VMEM((TILES, SUB, COLB * BLK), BF),
             pltpu.VMEM((TILES, SUB, COLB * BLK), BF),
             pltpu.VMEM((COLB, TILES, SUB, BLK), BF),
@@ -502,7 +490,7 @@
             pltpu.SMEM((8, LANE), jnp.int32),
             DMA, DMA, DMA((2,)), DMA((3,)), DMA((3,)),
             DMA, DMA, DMA, DMA, DMA((2,)), DMA, DMA((2,)), DMA, DMA, DMA, DMA, DMA((7,)), DMA((7,)),
-            DMA((4,)), DMA((3,)), DMA, DMA((7,)), DMA((6,)), DMA, DMA((4,)), pltpu.SemaphoreType.REGULAR,
+            DMA((4,)), DMA((3,)), DMA, DMA((7,)), DMA((6,)), DMA, DMA((2,)), pltpu.SemaphoreType.REGULAR,
         ],
         compiler_params=pltpu.CompilerParams(
             collective_id=0, has_side_effects=True, vmem_limit_bytes=58 * 1024 * 1024
@@ -517,23 +505,18 @@
         right_prev.reshape(2, 2 * HALF, SUB, BLK),
     )
 
-    rows_t = jax.ShapeDtypeStruct((TILES, 2, SUB, COLB * BLK), BF)
     sq = jax.ShapeDtypeStruct((2, BLK, BLK), F32)
+    results = [pltpu.with_memory_space_constraint(v, pltpu.VMEM) for v in (direction, left_new, right_new)]
     direction, left_new, right_new = pl.pallas_call(
-        finish_kernel,
-        out_shape=(rows_t, sq, sq),
-        in_specs=[SMEM, ANY, ANY, ANY, ANY],
+        store_kernel,
+        out_shape=(jax.ShapeDtypeStruct((TILES, 2, SUB, COLB * BLK), BF), sq, sq),
+        in_specs=[VMEM, VMEM, VMEM],
         out_specs=(ANY, ANY, ANY),
-        scratch_shapes=[
-            pltpu.VMEM((TILES, 2, SUB, COLB * BLK), BF),
-            pltpu.VMEM((HALF, 2, 2, SUB, BLK), BF),
-        ]
-        + [pltpu.VMEM((2, BLK, BLK), F32)] * 4
-        + [DMA((2,)), DMA((6,)), DMA((4,))],
-        compiler_params=pltpu.CompilerParams(vmem_limit_bytes=58 * 1024 * 1024),
-        cost_estimate=pl.CostEstimate(flops=4 * 2 * BLK**3, bytes_accessed=10 * 2**20, transcendentals=0),
-        name="new_factors",
-    )(block_owner, direction, gathered, left_prev, right_prev)
+        scratch_shapes=[DMA((5,))],
+        compiler_params=pltpu.CompilerParams(vmem_limit_bytes=16 * 1024 * 1024),
+        cost_estimate=pl.CostEstimate(flops=0, bytes_accessed=9 * 2**20, transcendentals=0),
+        name="store_results",
+    )(*results)
     return direction.reshape(rows, COLB * BLK), left_new, right_new
 
 

time: 57.8 us -> 54.3 us (0.939)
  Pallas kernels: 57.1 us -> 53.5 us
    pallas_call x2, Pallas kernels: 57.1 us -> 53.5 us  [the longest x1 51.3 us: body(): pl.pallas_call(step_kernel, out_shape=(pltpu.VMEM((TILES, 2, SUB, COLB *...]
where the time goes in v5:
time: 54.3 us; the launch traced here: 54.2 us
  Pallas kernels  53.5 us (99%)
  between operations  0.64 us (1%)
    pallas_call x1, Pallas kernels, body(): pl.pallas_call(step_kernel, out_shape=(pltpu.VMEM((TILES, 2, SUB, COLB *...  51.3 us
    pallas_call x1, Pallas kernels, body(): pl.pallas_call(store_kernel, out_shape=(jax.ShapeDtypeStruct((TILES, 2, S...  2.21 us

profile of v5, /device:TPU:1, one launch (start us, length us, event | category | flops | bytes accessed | tf_op | source)
XLA Modules:
  0.0 54.2 jit_solution(41970613400661810)
XLA Ops:
  0.6 51.3 %shampoo_step.1 = (bf16[5,2,16,1536]{3,2,1,0:T(8,128)(2,1)S(1)}, f32[2,512,512]{2,1,0:T(8,128)S(1)}, f32[2,512,512]{2,1,0:T(8,128)S(1)}) custom-call(s32[30]{0:T(128)} %block_owner.1, s32[30]{0:T(128)} %block_row.1, s32[30]{0:T(128)} %block_col.1, bf16[5,2,16,1536]{3,2,1,0:T(8,128)(2,1)} %bitcast.6, f32[2,32,16,512]{3,2,1,0:T(8,128)} %bitcast.4, ...), custom_call_target="tpu_custom_call" | custom-call | tf_op jit(solution)/shard_map/shampoo_step/pallas_call | solution.py:458
  52.0 2.2 %store_results.1 = (bf16[5,2,16,1536]{3,2,1,0:T(8,128)(2,1)}, f32[2,512,512]{2,1,0:T(8,128)}, f32[2,512,512]{2,1,0:T(8,128)}) custom-call(bf16[5,2,16,1536]{3,2,1,0:T(8,128)(2,1)S(1)} %get-tuple-element.9.d_in, f32[2,512,512]{2,1,0:T(8,128)S(1)} %get-tuple-element.10.left_in, f32[2,512,512]{2,1,0:T(8,128)S(1)} %get-tuple-element.11.right_in), custom_call_target="tpu_custom_call" | custom-call | bytes 9437184 | tf_op jit(solution)/shard_map/store_results/pallas_call | solution.py:510

commit v6 on v5

--- a/solution.py
+++ b/solution.py
@@ -86,9 +86,9 @@
 
 def step_kernel(
     block_owner, block_row, block_col, grads, left_prev, right_prev, d_out, left_out, right_out,
-    g_own, lp, rp, own, pair, part, xin, red, pvf, pvb, pm, po, pv, gc, mid, outb, acc, zb, scl, pb, full, tab, look,
+    g_own, lp, rp, own, pair, part, xin, red, xq, redq, pvf, pvb, pm, po, pv, gc, mid, outb, acc, zb, scl, pb, full, tab, look,
     own_sem, pvf_sem, pair_sem, xs_sem, xr_sem, p1_sem, p1r_sem, p2_sem, p2r_sem, gs_sem, gr_sem, ge_sem,
-    t1_sem, t1r_sem, t2_sem, t2r_sem, os_sem, or_sem, z_sem, ss_sem, sr_sem, ds_sem, dr_sem, tab_sem, in_sem, ready,
+    t1_sem, t1r_sem, t2_sem, t2r_sem, os_sem, or_sem, z_sem, ss_sem, sr_sem, ds_sem, dr_sem, tab_sem, in_sem, qs_sem, qr_sem, ready, rows_in,
 ):
     rep = lax.axis_index("rep")
     shard = lax.axis_index("shard")
@@ -101,7 +101,9 @@
     partner = 2 * x + 1 - h
     summing = x < COLB
     home = summing & (j == 1)
-    passing = half == h
+    place_h = (2 * w) // 3 - 3 * h
+    passing = (j != 1) & (place_h >= 0) & (place_h < 8)
+    passed_tile = jnp.where(passing, 8 * half + place_h, 0)
     lanes = pl.ds(pl.multiple_of(x * LANE, LANE), LANE)
     barrier = pltpu.get_barrier_semaphore()
 
@@ -143,7 +145,9 @@
     ]
     for copy in whole:
         copy.start()
-    loop(SHARDS - 1, lambda n: greet(barrier, rep, (shard + 1 + n) % SHARDS))
+    row0 = shard // 8 * 8
+    loop(7, lambda n: greet(barrier, rep, row0 + (shard + 1 + n) % 8))
+    loop(3, lambda n: greet(barrier, rep, (shard + 8 * n + 8) % SHARDS))
     for n in range(1, XS):
         greet(barrier, 2 * ((x + n) % XS) + h, shard)
     greet(barrier, partner, shard)
@@ -153,22 +157,46 @@
     arrived(pvf, pvf_sem)
     for n in range(2):
         pvb[:, n] = pvf[n].astype(BF)
-    pl.semaphore_wait(barrier, SHARDS - 1 + XS)
+    pl.semaphore_wait(barrier, 10 + XS)
 
     tables.wait()
     swap = send(grads.at[:, 1 - h], pair, pair_sem.at[0], pair_sem.at[1], partner, shard)
     swap.start()
+    def row_in(n):
+        pl.semaphore_signal(
+            rows_in, inc=1, device_id=(rep, (shard + 8 * n + 8) % SHARDS), device_id_type=MESH
+        )
+
+    loop(3, row_in)
+    pl.semaphore_wait(rows_in, 3)
     for n in range(1, XS):
         pl.semaphore_signal(
             ready, inc=1, device_id=(2 * ((x + n) % XS) + h, shard), device_id_type=MESH
         )
+    def taker(n):
+        e = n % 8
+        free = (3 * (e - 5 + 8 * (1 - h)) + 1) // 2
+        group = jnp.where(n < 8, x, (x + 1) % COLB)
+        to = HALF * (n // 8) + jnp.where(e < 5, 3 * e + 1, free)
+        return jnp.where(summing, 8 * group + e, n), jnp.where(summing, to, n)
+
+    free_place = (2 * w) // 3 - 8 * (1 - h)
+    old_here = jnp.logical_not(summing) | (j == 1) | ((free_place >= 0) & (free_place < 3))
+    old_place = jnp.where(summing, 8 * half + jnp.where(j == 1, r, 5 + free_place), shard)
+    old_place = jnp.where(old_here, old_place, 0)
+    old_tiles = jnp.where(summing, HALF, SHARDS)
+    old_first = jnp.where(old_here, old_place + 1, shard)
+    old_tile, _ = taker(old_place)
     mine = pm.at[pl.ds(2 * shard, 2)]
     def give_old(n):
-        t = (shard + 1 + n) % SHARDS
-        send(pvb.at[t], mine, p1_sem, p1r_sem, rep, t).start()
-
-    loop(SHARDS - 1, give_old)
-    pltpu.make_async_copy(pvb.at[shard], mine, p1r_sem).start()
+        t, to = taker((old_first + n) % old_tiles)
+        send(pvb.at[t], mine, p1_sem, p1r_sem, rep, to).start()
+
+    loop(old_tiles - old_here.astype(jnp.int32), give_old)
+
+    @pl.when(old_here)
+    def _():
+        pltpu.make_async_copy(pvb.at[old_tile], mine, p1r_sem).start()
 
     load.wait()
     swap.wait_recv()
@@ -182,31 +210,17 @@
             n = (c - x + XS) % XS - 1
             send(part.at[c], xin.at[n], xs_sem.at[c], xr_sem.at[n], 2 * c + h, shard).start()
 
-    arrived(pm, p1r_sem)
+    shares = []
+    for n in range(1, XS):
+        to = (x + n) % XS
+        cols = pl.ds(pl.multiple_of(to * LANE, LANE), LANE)
+        shares.append(
+            send(part.at[:, :, :, cols], xq.at[n - 1], qs_sem.at[n - 1], qr_sem.at[n - 1], 2 * to + h, shard)
+        )
+    for copy in shares:
+        copy.start()
+
     pl.semaphore_wait(ready, XS - 1)
-    tile_at_home = pv.at[shard, :, lanes]
-
-    def home_of(cell):
-        row = cell // COLB
-        return 2 * (cell % COLB) + h, HALF * (row // 5) + 3 * (row % 5) + 1
-
-    own_cell = COLB * (5 * half + r) + x
-    first = jnp.where(home, own_cell + 1, 0)
-
-    def give_factor(n):
-        cell = (first + n) % CELLS
-        po[cell] = pm[look[1, cell]]
-        to_rep, to_shard = home_of(cell)
-        send(po.at[cell], tile_at_home, p2_sem, p2r_sem, to_rep, to_shard).start()
-
-    loop(CELLS - home.astype(jnp.int32), give_factor)
-
-    @pl.when(home)
-    def _():
-        po[own_cell] = pm[look[1, own_cell]]
-        pltpu.make_async_copy(po.at[own_cell], tile_at_home, p2r_sem).start()
-
-
     def to_homes(act):
         @pl.when(j == 2)
         def _():
@@ -222,10 +236,10 @@
                     act(1, red.at[n:TILES], gc.at[0:TILES - n, h], shard + 1)
 
     def passing_tile(n):
-        u = TILES * w + n // XS
-        q = n % XS
-        src = red.at[n // XS, :, pl.ds(pl.multiple_of(q * LANE, LANE), LANE)]
-        return src, mid.at[COLB * (5 * half + u // HALF) + x], 2 * q + h, HALF * h + u % HALF
+        u = TILES * w + n
+        k = u % HALF
+        to = HALF * (k // 8) + (3 * (k % 8 + 3 * h) + 1) // 2
+        return redq.at[n], mid.at[pl.ds(COLB * (5 * half + u // HALF), COLB)], to
 
     @pl.when(summing)
     def _():
@@ -240,11 +254,42 @@
         def _():
             pltpu.make_async_copy(red, gc.at[pl.ds(TILES - r, TILES), h], gr_sem).start()
 
-        def give_tile(n):
-            src, dst, to_rep, to_shard = passing_tile(n)
-            pass_on(src, dst, t1_sem, t1r_sem, to_rep, to_shard)
-
-        loop(TILES * XS, give_tile)
+    tile_at_home = pv.at[old_tile, :, lanes]
+
+    def home_of(cell):
+        row = cell // COLB
+        return 2 * (cell % COLB) + h, HALF * (row // 5) + 3 * (row % 5) + 1
+
+    own_cell = COLB * (5 * half + r) + x
+    first = jnp.where(home, own_cell + 1, 0)
+
+    def give_factor(n):
+        cell = (first + n) % CELLS
+        po[cell] = pm[look[1, cell]]
+        to_rep, to_shard = home_of(cell)
+        send(po.at[cell], tile_at_home, p2_sem, p2r_sem, to_rep, to_shard).start()
+
+    @pl.when(old_here)
+    def _():
+        arrived(pm, p1r_sem)
+        loop(CELLS - home.astype(jnp.int32), give_factor)
+
+        @pl.when(home)
+        def _():
+            po[own_cell] = pm[look[1, own_cell]]
+            pltpu.make_async_copy(po.at[own_cell], tile_at_home, p2r_sem).start()
+
+
+    for copy in shares:
+        copy.wait_recv()
+    for c in range(COLB):
+        redq[:, c] = (
+            (part[c, :, :, lanes].astype(F32) + xq[0, c].astype(F32))
+            + (xq[1, c].astype(F32) + xq[2, c].astype(F32))
+        ).astype(BF)
+    for n in range(TILES):
+        src, dst, to = passing_tile(n)
+        pass_on(src, dst, t1_sem, t1r_sem, rep, to)
 
     half_block = send(gc.at[:, h], gc.at[:, h], ge_sem.at[0], ge_sem.at[1], partner, shard)
 
@@ -255,6 +300,9 @@
 
     def view(hh, col):
         return g_own.at[:, :, hh, :, pl.ds(pl.multiple_of(col * LANE, LANE), LANE)]
+
+    def slot_view(slot, hh, col):
+        return g_own.at[:, slot, hh, :, pl.ds(pl.multiple_of(col * LANE, LANE), LANE)]
 
     @pl.when(passing)
     def _():
@@ -264,7 +312,7 @@
             for n in range(2):
                 outb[o, n] = mid[look[0, 2 * o + n]]
 
-        slots_at_owner = g_own.at[w, :, h, :, lanes]
+        slots_at_owner = g_own.at[passed_tile, :, h, :, lanes]
 
         def give_slots(n):
             o = (shard + 1 + n) % SHARDS
@@ -289,7 +337,8 @@
         arrived(other, ge_sem.at[1])
         g = gc[...].reshape(BLK, BLK)
         gt = g.T
-        arrived(pv, p2r_sem)
+        gf = g.astype(F32)
+        sg = jnp.full((8, LANE), jnp.sum(gf * gf), F32)
 
         @pl.when(h == 0)
         def _():
@@ -299,14 +348,16 @@
         def _():
             acc[...] = mm(gt, g)
 
+        arrived(pv.at[0:20], p2r_sem)
+        for a, b in ((2, 0), (0, 1), (1, 2), (3, 0), (3, 1), (3, 2)):
+            there = pv[8 * b:8 * b + 8, :, a * LANE:(a + 1) * LANE].reshape(LANE, LANE)
+            pv[8 * a:8 * a + 8, :, b * LANE:(b + 1) * LANE] = there.T.reshape(8, SUB, LANE)
         val = acc[...] + pv[...].reshape(BLK, BLK).astype(F32)
         scale = jnp.sum(jnp.where(eye(BLK), val, 0.0)) * (1.0 / BLK)
         zb[h] = root_less_one(val, scale)
         scl[h] = lax.rsqrt(jnp.sqrt(jnp.full((8, LANE), scale, F32)))
         root.start()
         root_scale.start()
-        gf = g.astype(F32)
-        sg = jnp.full((8, LANE), jnp.sum(gf * gf), F32)
         arrived(zb.at[1 - h], z_sem.at[1])
         arrived(scl.at[1 - h], z_sem.at[3])
         y = scl[0, 0:1, 0:1] * (gf + mm(zb[0], g))
@@ -321,12 +372,14 @@
                 to_rows(lambda i, src, dst, to: send(src, dst, ss_sem.at[i], sr_sem, rep, to).start(), n)
                 pltpu.make_async_copy(pb.at[5 - n:10 - n, h], full.at[x, :, h], sr_sem).start()
 
-    owned = view(h, x)
-    arrived(owned, t2r_sem)
+    arrived(view(h, x), t2r_sem)
     outs = []
-    for n in (2, 1, 3):
-        outs.append(send(owned, owned, os_sem.at[n], or_sem.at[n], 2 * ((x + n) % XS) + h, shard))
-    outs.append(send(owned, owned, os_sem.at[0], or_sem.at[0], partner, shard))
+    for slot in range(2):
+        owned = slot_view(slot, h, x)
+        for n in (2, 1, 3):
+            to = 2 * ((x + n) % XS) + h
+            outs.append(send(owned, owned, os_sem.at[7 * slot + n], or_sem.at[7 * slot + n], to, shard))
+        outs.append(send(owned, owned, os_sem.at[7 * slot], or_sem.at[7 * slot], partner, shard))
     for copy in outs:
         copy.start()
 
@@ -342,12 +395,16 @@
         for copy in row_sends:
             copy.start()
 
-    for n in (1, 3, 2):
-        piece = view(h, (x + XS - n) % XS)
-        arrived(piece, or_sem.at[n])
-        copy = send(piece, piece, os_sem.at[3 + n], or_sem.at[3 + n], partner, shard)
-        copy.start()
-        outs.append(copy)
+    def to_partner(slot):
+        for n in (1, 3, 2):
+            piece = slot_view(slot, h, (x + XS - n) % XS)
+            arrived(piece, or_sem.at[7 * slot + n])
+            sem = 7 * slot + 3 + n
+            copy = send(piece, piece, os_sem.at[sem], or_sem.at[sem], partner, shard)
+            copy.start()
+            outs.append(copy)
+
+    to_partner(0)
 
     def onward(c):
         return send(
@@ -361,12 +418,13 @@
             arrived(full.at[c, :, h], dr_sem.at[c])
             onward(c).start()
 
-    for index, n in ((0, 0), (4, 1), (6, 3), (5, 2)):
-        arrived(view(1 - h, (x + XS - n) % XS), or_sem.at[index])
+    to_partner(1)
     for copy in whole:
         copy.wait()
 
     def factors(n):
+        for index, m in ((0, 0), (4, 1), (6, 3), (5, 2)):
+            arrived(slot_view(n, 1 - h, (x + XS - m) % XS), or_sem.at[7 * n + index])
         on = look[2, 2 * shard + n] > 0
         g = g_own[:, n].reshape(BLK, BLK)
         g = jnp.where(on, g, jnp.zeros_like(g))
@@ -375,19 +433,36 @@
             new = prev[n].reshape(BLK, BLK) + mm(a, b)
             out[n] = jnp.where(on, new, jnp.zeros_like(new))
 
-    loop(2, factors)
+    for n in range(2):
+        factors(n)
     for c in range(COLB):
         arrived(full.at[c, :, 1 - h], dr_sem.at[COLB + c])
         d_out[:, :, :, c * BLK:(c + 1) * BLK] = full[c]
 
+    kept = passing & ((passed_tile - TILES * w + 5 * HALF) % HALF < TILES)
+
+    @pl.when(kept)
+    def _():
+        arrived(mid.at[0:COLB * (TILES - 1)], t1_sem)
+
+    @pl.when(jnp.logical_not(kept))
+    def _():
+        arrived(mid.at[0:COLB * TILES], t1_sem)
+
+    for copy in shares:
+        copy.wait_send()
     swap.wait_send()
-    arrived(pvb.at[0:SHARDS - 1], p1_sem)
-
-    @pl.when(home)
+    for count, kept in ((16, 0), (16, 1), (32, 1)):
+
+        @pl.when((old_tiles == count) & (old_here.astype(jnp.int32) == kept))
+        def _():
+            arrived(pvb.at[0:count - kept], p1_sem)
+
+    @pl.when(old_here & home)
     def _():
         arrived(po.at[0:CELLS - 1], p2_sem)
 
-    @pl.when(jnp.logical_not(home))
+    @pl.when(old_here & jnp.logical_not(home))
     def _():
         arrived(po, p2_sem)
 
@@ -402,16 +477,6 @@
     @pl.when(summing)
     def _():
         to_homes(lambda n, src, dst, to: send(src, dst, gs_sem.at[n], gr_sem, rep, to).wait_send())
-
-        kept = passing & ((12 * w) % HALF < TILES)
-
-        @pl.when(kept)
-        def _():
-            arrived(mid.at[0:TILES * XS - 1], t1_sem)
-
-        @pl.when(jnp.logical_not(kept))
-        def _():
-            arrived(mid.at[0:TILES * XS], t1_sem)
 
         for copy in row_sends:
             copy.wait_send()
@@ -473,6 +538,8 @@
             pltpu.VMEM((COLB, TILES, SUB, BLK), BF),
             pltpu.VMEM((XS - 1, TILES, SUB, BLK), BF),
             pltpu.VMEM((TILES, SUB, BLK), BF),
+            pltpu.VMEM((XS - 1, COLB, TILES, SUB, LANE), BF),
+            pltpu.VMEM((TILES, COLB, SUB, LANE), BF),
             pltpu.VMEM((2, 2 * HALF, SUB, LANE), F32),
             pltpu.VMEM((2 * HALF, 2, SUB, LANE), BF),
             pltpu.VMEM((2 * SHARDS, SUB, LANE), BF),
@@ -489,8 +556,8 @@
             pltpu.VMEM((8, LANE), jnp.int32),
             pltpu.SMEM((8, LANE), jnp.int32),
             DMA, DMA, DMA((2,)), DMA((3,)), DMA((3,)),
-            DMA, DMA, DMA, DMA, DMA((2,)), DMA, DMA((2,)), DMA, DMA, DMA, DMA, DMA((7,)), DMA((7,)),
-            DMA((4,)), DMA((3,)), DMA, DMA((7,)), DMA((6,)), DMA, DMA((2,)), pltpu.SemaphoreType.REGULAR,
+            DMA, DMA, DMA, DMA, DMA((2,)), DMA, DMA((2,)), DMA, DMA, DMA, DMA, DMA((14,)), DMA((14,)),
+            DMA((4,)), DMA((3,)), DMA, DMA((7,)), DMA((6,)), DMA, DMA((2,)), DMA((3,)), DMA((3,)), pltpu.SemaphoreType.REGULAR, pltpu.SemaphoreType.REGULAR,
         ],
         compiler_params=pltpu.CompilerParams(
             collective_id=0, has_side_effects=True, vmem_limit_bytes=58 * 1024 * 1024

time: 54.3 us -> 49.9 us (0.919); the launches traced: 54.2 us -> 49 us
  Pallas kernels: 53.5 us -> 48.4 us
    pallas_call x1, Pallas kernels: 51.3 us -> 46.2 us  [body(): pl.pallas_call(step_kernel, out_shape=(pltpu.VMEM((TILES, 2, SUB, COLB *...]
where the time goes in v6:
time: 49.9 us; the launch traced here: 49 us
  Pallas kernels  48.4 us (97%)
  between operations  0.64 us (1%)
    pallas_call x1, Pallas kernels, body(): pl.pallas_call(step_kernel, out_shape=(pltpu.VMEM((TILES, 2, SUB, COLB *...  46.2 us
    pallas_call x1, Pallas kernels, body(): pl.pallas_call(store_kernel, out_shape=(jax.ShapeDtypeStruct((TILES, 2, S...  2.21 us

profile of v6, /device:TPU:1, one launch (start us, length us, event | category | flops | bytes accessed | tf_op | source)
XLA Modules:
  0.0 49.0 jit_solution(8856264687468741238)
XLA Ops:
  0.6 46.2 %shampoo_step.1 = (bf16[5,2,16,1536]{3,2,1,0:T(8,128)(2,1)S(1)}, f32[2,512,512]{2,1,0:T(8,128)S(1)}, f32[2,512,512]{2,1,0:T(8,128)S(1)}) custom-call(s32[30]{0:T(128)} %block_owner.1, s32[30]{0:T(128)} %block_row.1, s32[30]{0:T(128)} %block_col.1, bf16[5,2,16,1536]{3,2,1,0:T(8,128)(2,1)} %bitcast.6, f32[2,32,16,512]{3,2,1,0:T(8,128)} %bitcast.4, ...), custom_call_target="tpu_custom_call" | custom-call | tf_op jit(solution)/shard_map/shampoo_step/pallas_call | solution.py:523
  46.8 2.2 %store_results.1 = (bf16[5,2,16,1536]{3,2,1,0:T(8,128)(2,1)}, f32[2,512,512]{2,1,0:T(8,128)}, f32[2,512,512]{2,1,0:T(8,128)}) custom-call(bf16[5,2,16,1536]{3,2,1,0:T(8,128)(2,1)S(1)} %get-tuple-element.9.d_in, f32[2,512,512]{2,1,0:T(8,128)S(1)} %get-tuple-element.10.left_in, f32[2,512,512]{2,1,0:T(8,128)S(1)} %get-tuple-element.11.right_in), custom_call_target="tpu_custom_call" | custom-call | bytes 9437184 | tf_op jit(solution)/shard_map/store_results/pallas_call | solution.py:577

commit v7 on v6

--- a/solution.py
+++ b/solution.py
@@ -61,8 +61,7 @@
     ub = u.astype(BF)
     v = 2.0 * u + mm(ub, ub)
     w = 4.0 * u - 5.0 * e
-    z = (u - 0.25 * v) + 0.25 * mm(v.astype(BF), w.astype(BF))
-    return z.astype(BF)
+    return u - 0.25 * v, v.astype(BF), w.astype(BF)
 
 
 def fill_tables(tab, block_owner, block_row, block_col):
@@ -100,10 +99,20 @@
     j = w % 3
     partner = 2 * x + 1 - h
     summing = x < COLB
-    home = summing & (j == 1)
-    place_h = (2 * w) // 3 - 3 * h
-    passing = (j != 1) & (place_h >= 0) & (place_h < 8)
-    passed_tile = jnp.where(passing, 8 * half + place_h, 0)
+    home_row = ((j == 1) & (r < 3)) | ((j == 2) & (r >= 3))
+    home = summing & home_row
+    number = w
+    for n in (1, 4, 7, 11, 14):
+        number = number - (w > n).astype(jnp.int32)
+    passing = jnp.logical_not(home_row) & (number >= 3 * h) & (number < 3 * h + 8)
+
+    def numbered(n):
+        return (3 * n + 1 - (n > 6).astype(jnp.int32)) // 2
+
+    def home_shard(group):
+        return 3 * group + 1 + (group > 2).astype(jnp.int32)
+
+    passed_tile = jnp.where(passing, 8 * half + number - 3 * h, 0)
     lanes = pl.ds(pl.multiple_of(x * LANE, LANE), LANE)
     barrier = pltpu.get_barrier_semaphore()
 
@@ -128,38 +137,32 @@
 
         lax.fori_loop(0, count, step, 0)
 
-    load = pltpu.make_async_copy(grads.at[:, h], own, own_sem)
-    load.start()
-
-    @pl.when(h == 0)
-    def _():
-        pltpu.make_async_copy(left_prev.at[:, :, :, lanes], pvf, pvf_sem).start()
-
-    @pl.when(h == 1)
-    def _():
-        pltpu.make_async_copy(right_prev.at[:, :, :, lanes], pvf, pvf_sem).start()
-
-    whole = [
-        pltpu.make_async_copy(left_prev, lp, in_sem.at[0]),
-        pltpu.make_async_copy(right_prev, rp, in_sem.at[1]),
-    ]
-    for copy in whole:
-        copy.start()
     row0 = shard // 8 * 8
     loop(7, lambda n: greet(barrier, rep, row0 + (shard + 1 + n) % 8))
     loop(3, lambda n: greet(barrier, rep, (shard + 8 * n + 8) % SHARDS))
     for n in range(1, XS):
         greet(barrier, 2 * ((x + n) % XS) + h, shard)
     greet(barrier, partner, shard)
-    fill_tables(tab, block_owner, block_row, block_col)
-    tables = pltpu.make_async_copy(tab, look, tab_sem)
-    tables.start()
+    load = pltpu.make_async_copy(grads.at[:, h], own, own_sem)
+    load.start()
+
+    @pl.when(h == 0)
+    def _():
+        pltpu.make_async_copy(left_prev.at[:, :, :, lanes], pvf, pvf_sem).start()
+
+    @pl.when(h == 1)
+    def _():
+        pltpu.make_async_copy(right_prev.at[:, :, :, lanes], pvf, pvf_sem).start()
+
+    whole = [
+        pltpu.make_async_copy(left_prev, lp, in_sem.at[0]),
+        pltpu.make_async_copy(right_prev, rp, in_sem.at[1]),
+    ]
     arrived(pvf, pvf_sem)
     for n in range(2):
         pvb[:, n] = pvf[n].astype(BF)
     pl.semaphore_wait(barrier, 10 + XS)
 
-    tables.wait()
     swap = send(grads.at[:, 1 - h], pair, pair_sem.at[0], pair_sem.at[1], partner, shard)
     swap.start()
     def row_in(n):
@@ -175,14 +178,14 @@
         )
     def taker(n):
         e = n % 8
-        free = (3 * (e - 5 + 8 * (1 - h)) + 1) // 2
+        free = numbered(jnp.maximum(e - 5 + 8 * (1 - h), 0))
         group = jnp.where(n < 8, x, (x + 1) % COLB)
-        to = HALF * (n // 8) + jnp.where(e < 5, 3 * e + 1, free)
+        to = HALF * (n // 8) + jnp.where(e < 5, home_shard(e), free)
         return jnp.where(summing, 8 * group + e, n), jnp.where(summing, to, n)
 
-    free_place = (2 * w) // 3 - 8 * (1 - h)
-    old_here = jnp.logical_not(summing) | (j == 1) | ((free_place >= 0) & (free_place < 3))
-    old_place = jnp.where(summing, 8 * half + jnp.where(j == 1, r, 5 + free_place), shard)
+    free_place = number - 8 * (1 - h)
+    old_here = jnp.logical_not(summing) | home_row | ((free_place >= 0) & (free_place < 3))
+    old_place = jnp.where(summing, 8 * half + jnp.where(home_row, r, 5 + free_place), shard)
     old_place = jnp.where(old_here, old_place, 0)
     old_tiles = jnp.where(summing, HALF, SHARDS)
     old_first = jnp.where(old_here, old_place + 1, shard)
@@ -198,18 +201,16 @@
     def _():
         pltpu.make_async_copy(pvb.at[old_tile], mine, p1r_sem).start()
 
+    fill_tables(tab, block_owner, block_row, block_col)
+    tables = pltpu.make_async_copy(tab, look, tab_sem)
+    tables.start()
+    for copy in whole:
+        copy.start()
     load.wait()
     swap.wait_recv()
     for c in range(COLB):
         cols = slice(c * BLK, (c + 1) * BLK)
         part[c] = (own[:, :, cols].astype(F32) + pair[:, :, cols].astype(F32)).astype(BF)
-    for c in range(COLB):
-
-        @pl.when(x != c)
-        def _():
-            n = (c - x + XS) % XS - 1
-            send(part.at[c], xin.at[n], xs_sem.at[c], xr_sem.at[n], 2 * c + h, shard).start()
-
     shares = []
     for n in range(1, XS):
         to = (x + n) % XS
@@ -220,45 +221,44 @@
     for copy in shares:
         copy.start()
 
+    for c in range(COLB):
+
+        @pl.when(x != c)
+        def _():
+            n = (c - x + XS) % XS - 1
+            send(part.at[c], xin.at[n], xs_sem.at[c], xr_sem.at[n], 2 * c + h, shard).start()
+
+    tables.wait()
     pl.semaphore_wait(ready, XS - 1)
     def to_homes(act):
-        @pl.when(j == 2)
+        @pl.when((j == 2) & (r < 3))
         def _():
             act(0, red, gc.at[pl.ds(10 - r, TILES), h], shard - 1)
+
+        @pl.when((j == 1) & (r >= 3))
+        def _():
+            act(0, red, gc.at[pl.ds(TILES - r, TILES), h], shard + 1)
 
         for n in range(6):
 
             @pl.when((j == 0) & (r == n))
             def _():
                 if n > 0:
-                    act(0, red.at[0:n], gc.at[16 - n:16, h], shard - 2)
+                    act(0, red.at[0:n], gc.at[16 - n:16, h], shard - (2 if n < 4 else 1))
                 if n < TILES:
-                    act(1, red.at[n:TILES], gc.at[0:TILES - n, h], shard + 1)
+                    act(1, red.at[n:TILES], gc.at[0:TILES - n, h], shard + (1 if n < 3 else 2))
 
     def passing_tile(n):
         u = TILES * w + n
         k = u % HALF
-        to = HALF * (k // 8) + (3 * (k % 8 + 3 * h) + 1) // 2
+        to = HALF * (k // 8) + numbered(k % 8 + 3 * h)
         return redq.at[n], mid.at[pl.ds(COLB * (5 * half + u // HALF), COLB)], to
-
-    @pl.when(summing)
-    def _():
-        for n in range(XS - 1):
-            arrived(xin.at[n], xr_sem.at[n])
-        red[...] = (
-            (part[x].astype(F32) + xin[0].astype(F32)) + (xin[1].astype(F32) + xin[2].astype(F32))
-        ).astype(BF)
-        to_homes(lambda n, src, dst, to: send(src, dst, gs_sem.at[n], gr_sem, rep, to).start())
-
-        @pl.when(j == 1)
-        def _():
-            pltpu.make_async_copy(red, gc.at[pl.ds(TILES - r, TILES), h], gr_sem).start()
 
     tile_at_home = pv.at[old_tile, :, lanes]
 
     def home_of(cell):
         row = cell // COLB
-        return 2 * (cell % COLB) + h, HALF * (row // 5) + 3 * (row % 5) + 1
+        return 2 * (cell % COLB) + h, HALF * (row // 5) + home_shard(row % 5)
 
     own_cell = COLB * (5 * half + r) + x
     first = jnp.where(home, own_cell + 1, 0)
@@ -291,6 +291,19 @@
         src, dst, to = passing_tile(n)
         pass_on(src, dst, t1_sem, t1r_sem, rep, to)
 
+    @pl.when(summing)
+    def _():
+        for n in range(XS - 1):
+            arrived(xin.at[n], xr_sem.at[n])
+        red[...] = (
+            (part[x].astype(F32) + xin[0].astype(F32)) + (xin[1].astype(F32) + xin[2].astype(F32))
+        ).astype(BF)
+        to_homes(lambda n, src, dst, to: send(src, dst, gs_sem.at[n], gr_sem, rep, to).start())
+
+        @pl.when(home)
+        def _():
+            pltpu.make_async_copy(red, gc.at[pl.ds(TILES * j - r, TILES), h], gr_sem).start()
+
     half_block = send(gc.at[:, h], gc.at[:, h], ge_sem.at[0], ge_sem.at[1], partner, shard)
 
     @pl.when(home)
@@ -323,13 +336,21 @@
         fill(shard)
         pltpu.make_async_copy(outb.at[shard], slots_at_owner, t2r_sem).start()
 
-    root = send(zb.at[h], zb.at[h], z_sem.at[0], z_sem.at[1], partner, shard)
-    root_scale = send(scl.at[h], scl.at[h], z_sem.at[2], z_sem.at[3], partner, shard)
+    halves = (pl.ds(0, BLK // 2), pl.ds(BLK // 2, BLK // 2))
+    roots = [
+        send(zb.at[h, rows], zb.at[h, rows], z_sem.at[n], z_sem.at[3 + n], partner, shard)
+        for n, rows in enumerate(halves)
+    ]
+    roots.append(send(scl.at[h], scl.at[h], z_sem.at[2], z_sem.at[5], partner, shard))
 
     def to_rows(act, n):
-        act(0, pb.at[0:TILES - n, h], full.at[x, n:TILES, h], shard - 1)
-        act(1, pb.at[10 - n:15 - n, h], full.at[x, :, h], shard + 1)
-        act(2, pb.at[15 - n:16, h], full.at[x, 0:1 + n, h], shard + 2)
+        early = n < 3
+        act(0, pb.at[0:TILES - n, h], full.at[x, n:TILES, h], shard - (1 if early else 2))
+        if early:
+            act(1, pb.at[10 - n:15 - n, h], full.at[x, :, h], shard + 1)
+        else:
+            act(1, pb.at[5 - n:10 - n, h], full.at[x, :, h], shard - 1)
+        act(2, pb.at[15 - n:16, h], full.at[x, 0:1 + n, h], shard + (2 if early else 1))
 
     @pl.when(home)
     def _():
@@ -354,14 +375,36 @@
             pv[8 * a:8 * a + 8, :, b * LANE:(b + 1) * LANE] = there.T.reshape(8, SUB, LANE)
         val = acc[...] + pv[...].reshape(BLK, BLK).astype(F32)
         scale = jnp.sum(jnp.where(eye(BLK), val, 0.0)) * (1.0 / BLK)
-        zb[h] = root_less_one(val, scale)
         scl[h] = lax.rsqrt(jnp.sqrt(jnp.full((8, LANE), scale, F32)))
-        root.start()
-        root_scale.start()
-        arrived(zb.at[1 - h], z_sem.at[1])
-        arrived(scl.at[1 - h], z_sem.at[3])
-        y = scl[0, 0:1, 0:1] * (gf + mm(zb[0], g))
-        p = scl[1, 0:1, 0:1] * (y + mm(y.astype(BF), zb[1]))
+        roots[2].start()
+        rest, v, u = root_less_one(val, scale)
+        for n, rows in enumerate(halves):
+            part_v = v[n * (BLK // 2):(n + 1) * (BLK // 2)]
+            zb[h, rows] = (rest[n * (BLK // 2):(n + 1) * (BLK // 2)] + 0.25 * mm(part_v, u)).astype(BF)
+            roots[n].start()
+
+        @pl.when(h == 0)
+        def _():
+            acc[...] = scl[0, 0:1, 0:1] * (gf + mm(zb[0], g))
+
+        @pl.when(h == 1)
+        def _():
+            acc[...] = scl[1, 0:1, 0:1] * (gf + mm(g, zb[1]))
+
+        y = acc[...]
+        for n, rows in enumerate(halves):
+            arrived(zb.at[1 - h, rows], z_sem.at[3 + n])
+        arrived(scl.at[1 - h], z_sem.at[5])
+
+        @pl.when(h == 0)
+        def _():
+            acc[...] = scl[1, 0:1, 0:1] * (y + mm(y.astype(BF), zb[1]))
+
+        @pl.when(h == 1)
+        def _():
+            acc[...] = scl[0, 0:1, 0:1] * (y + mm(zb[0], y.astype(BF)))
+
+        p = acc[...]
         sp = jnp.full((8, LANE), jnp.sum(p * p), F32)
         ratio = jnp.sqrt(sg / (sp + 1e-06))[0:1, 0:1]
         pb[...] = (p * ratio).astype(BF).reshape(HALF, 2, SUB, BLK)
@@ -370,7 +413,8 @@
             @pl.when(r == n)
             def _():
                 to_rows(lambda i, src, dst, to: send(src, dst, ss_sem.at[i], sr_sem, rep, to).start(), n)
-                pltpu.make_async_copy(pb.at[5 - n:10 - n, h], full.at[x, :, h], sr_sem).start()
+                at = (5 if n < 3 else 10) - n
+                pltpu.make_async_copy(pb.at[at:at + TILES, h], full.at[x, :, h], sr_sem).start()
 
     arrived(view(h, x), t2r_sem)
     outs = []
@@ -488,8 +532,8 @@
     @pl.when(home)
     def _():
         half_block.wait_send()
-        root.wait_send()
-        root_scale.wait_send()
+        for copy in roots:
+            copy.wait_send()
         for n in range(TILES):
 
             @pl.when(r == n)
@@ -557,7 +601,7 @@
             pltpu.SMEM((8, LANE), jnp.int32),
             DMA, DMA, DMA((2,)), DMA((3,)), DMA((3,)),
             DMA, DMA, DMA, DMA, DMA((2,)), DMA, DMA((2,)), DMA, DMA, DMA, DMA, DMA((14,)), DMA((14,)),
-            DMA((4,)), DMA((3,)), DMA, DMA((7,)), DMA((6,)), DMA, DMA((2,)), DMA((3,)), DMA((3,)), pltpu.SemaphoreType.REGULAR, pltpu.SemaphoreType.REGULAR,
+            DMA((6,)), DMA((3,)), DMA, DMA((7,)), DMA((6,)), DMA, DMA((2,)), DMA((3,)), DMA((3,)), pltpu.SemaphoreType.REGULAR, pltpu.SemaphoreType.REGULAR,
         ],
         compiler_params=pltpu.CompilerParams(
             collective_id=0, has_side_effects=True, vmem_limit_bytes=58 * 1024 * 1024

time: 49.9 us -> 49.1 us (0.984); the launches traced: 49 us -> 49 us
  no operation moved by 1% of the time
where the time goes in v7:
time: 49.1 us; the launch traced here: 49 us
  Pallas kernels  48.3 us (98%)
  between operations  0.64 us (1%)
    pallas_call x1, Pallas kernels, body(): pl.pallas_call(step_kernel, out_shape=(pltpu.VMEM((TILES, 2, SUB, COLB *...  46.1 us
    pallas_call x1, Pallas kernels, body(): pl.pallas_call(store_kernel, out_shape=(jax.ShapeDtypeStruct((TILES, 2, S...  2.21 us

profile of v7, /device:TPU:1, one launch (start us, length us, event | category | flops | bytes accessed | tf_op | source)
XLA Modules:
  0.0 49.0 jit_solution(4437049531635191931)
XLA Ops:
  0.6 46.1 %shampoo_step.1 = (bf16[5,2,16,1536]{3,2,1,0:T(8,128)(2,1)S(1)}, f32[2,512,512]{2,1,0:T(8,128)S(1)}, f32[2,512,512]{2,1,0:T(8,128)S(1)}) custom-call(s32[30]{0:T(128)} %block_owner.1, s32[30]{0:T(128)} %block_row.1, s32[30]{0:T(128)} %block_col.1, bf16[5,2,16,1536]{3,2,1,0:T(8,128)(2,1)} %bitcast.6, f32[2,32,16,512]{3,2,1,0:T(8,128)} %bitcast.4, ...), custom_call_target="tpu_custom_call" | custom-call | tf_op jit(solution)/shard_map/shampoo_step/pallas_call | solution.py:567
  46.8 2.2 %store_results.1 = (bf16[5,2,16,1536]{3,2,1,0:T(8,128)(2,1)}, f32[2,512,512]{2,1,0:T(8,128)}, f32[2,512,512]{2,1,0:T(8,128)}) custom-call(bf16[5,2,16,1536]{3,2,1,0:T(8,128)(2,1)S(1)} %get-tuple-element.9.d_in, f32[2,512,512]{2,1,0:T(8,128)S(1)} %get-tuple-element.10.left_in, f32[2,512,512]{2,1,0:T(8,128)S(1)} %get-tuple-element.11.right_in), custom_call_target="tpu_custom_call" | custom-call | bytes 9437184 | tf_op jit(solution)/shard_map/store_results/pallas_call | solution.py:621

commit v8 on v7

--- a/solution.py
+++ b/solution.py
@@ -99,11 +99,17 @@
     j = w % 3
     partner = 2 * x + 1 - h
     summing = x < COLB
-    home_row = ((j == 1) & (r < 3)) | ((j == 2) & (r >= 3))
+    def spot(a_shard):
+        at = a_shard % HALF
+        group, side = at // 3, at % 3
+        is_home = ((side == 1) & (group < 3)) | ((side == 2) & (group >= 3))
+        number = at
+        for n in (1, 4, 7, 11, 14):
+            number = number - (at > n).astype(jnp.int32)
+        return a_shard // HALF, group, is_home, number
+
+    _, _, home_row, number = spot(shard)
     home = summing & home_row
-    number = w
-    for n in (1, 4, 7, 11, 14):
-        number = number - (w > n).astype(jnp.int32)
     passing = jnp.logical_not(home_row) & (number >= 3 * h) & (number < 3 * h + 8)
 
     def numbered(n):
@@ -136,6 +142,12 @@
             return carry
 
         lax.fori_loop(0, count, step, 0)
+
+    def far(n):
+        i, m = n // 4, n % 4
+        dz = 4 + jnp.where(i % 2 == 0, i // 2, -((i + 1) // 2))
+        dy = 2 + jnp.where(m % 2 == 0, m // 2, -((m + 1) // 2))
+        return (shard // 8 + dy) % 4 * 8 + (shard % 8 + dz) % 8
 
     row0 = shard // 8 * 8
     loop(7, lambda n: greet(barrier, rep, row0 + (shard + 1 + n) % 8))
@@ -176,26 +188,24 @@
         pl.semaphore_signal(
             ready, inc=1, device_id=(2 * ((x + n) % XS) + h, shard), device_id_type=MESH
         )
-    def taker(n):
-        e = n % 8
-        free = numbered(jnp.maximum(e - 5 + 8 * (1 - h), 0))
-        group = jnp.where(n < 8, x, (x + 1) % COLB)
-        to = HALF * (n // 8) + jnp.where(e < 5, home_shard(e), free)
-        return jnp.where(summing, 8 * group + e, n), jnp.where(summing, to, n)
-
-    free_place = number - 8 * (1 - h)
-    old_here = jnp.logical_not(summing) | home_row | ((free_place >= 0) & (free_place < 3))
-    old_place = jnp.where(summing, 8 * half + jnp.where(home_row, r, 5 + free_place), shard)
-    old_place = jnp.where(old_here, old_place, 0)
-    old_tiles = jnp.where(summing, HALF, SHARDS)
-    old_first = jnp.where(old_here, old_place + 1, shard)
-    old_tile, _ = taker(old_place)
+    def taker(a_shard):
+        of, group, is_home, number = spot(a_shard)
+        free = number - 8 * (1 - h)
+        here = jnp.logical_not(summing) | is_home | ((free >= 0) & (free < 3))
+        rows = 8 * jnp.where(of == 0, x, (x + 1) % COLB) + jnp.where(is_home, group, 5 + free)
+        return here, jnp.where(here, jnp.where(summing, rows, a_shard), 0)
+
+    old_here, old_tile = taker(shard)
     mine = pm.at[pl.ds(2 * shard, 2)]
     def give_old(n):
-        t, to = taker((old_first + n) % old_tiles)
-        send(pvb.at[t], mine, p1_sem, p1r_sem, rep, to).start()
-
-    loop(old_tiles - old_here.astype(jnp.int32), give_old)
+        to = far(n)
+        here, t = taker(to)
+
+        @pl.when(here)
+        def _():
+            send(pvb.at[t], mine, p1_sem, p1r_sem, rep, to).start()
+
+    loop(SHARDS - 1, give_old)
 
     @pl.when(old_here)
     def _():
@@ -256,28 +266,28 @@
 
     tile_at_home = pv.at[old_tile, :, lanes]
 
-    def home_of(cell):
-        row = cell // COLB
-        return 2 * (cell % COLB) + h, HALF * (row // 5) + home_shard(row % 5)
-
-    own_cell = COLB * (5 * half + r) + x
-    first = jnp.where(home, own_cell + 1, 0)
-
-    def give_factor(n):
-        cell = (first + n) % CELLS
-        po[cell] = pm[look[1, cell]]
-        to_rep, to_shard = home_of(cell)
-        send(po.at[cell], tile_at_home, p2_sem, p2r_sem, to_rep, to_shard).start()
+    def give_group(to, start):
+        of, group, _, _ = spot(to)
+        for c in range(COLB):
+            cell = COLB * (5 * of + group) + c
+            po[cell] = pm[look[1, cell]]
+            start(po.at[cell], tile_at_home, p2_sem, p2r_sem, 2 * c + h, to)
+
+    def give_factors(n):
+        to = far(n)
+
+        @pl.when(spot(to)[2])
+        def _():
+            give_group(to, lambda *args: send(*args).start())
 
     @pl.when(old_here)
     def _():
         arrived(pm, p1r_sem)
-        loop(CELLS - home.astype(jnp.int32), give_factor)
-
-        @pl.when(home)
-        def _():
-            po[own_cell] = pm[look[1, own_cell]]
-            pltpu.make_async_copy(po.at[own_cell], tile_at_home, p2r_sem).start()
+        loop(SHARDS - 1, give_factors)
+
+        @pl.when(home_row)
+        def _():
+            give_group(shard, pass_on)
 
 
     for copy in shares:
@@ -314,9 +324,6 @@
     def view(hh, col):
         return g_own.at[:, :, hh, :, pl.ds(pl.multiple_of(col * LANE, LANE), LANE)]
 
-    def slot_view(slot, hh, col):
-        return g_own.at[:, slot, hh, :, pl.ds(pl.multiple_of(col * LANE, LANE), LANE)]
-
     @pl.when(passing)
     def _():
         arrived(mid, t1r_sem)
@@ -328,7 +335,7 @@
         slots_at_owner = g_own.at[passed_tile, :, h, :, lanes]
 
         def give_slots(n):
-            o = (shard + 1 + n) % SHARDS
+            o = far(n)
             fill(o)
             send(outb.at[o], slots_at_owner, t2_sem, t2r_sem, rep, o).start()
 
@@ -416,14 +423,12 @@
                 at = (5 if n < 3 else 10) - n
                 pltpu.make_async_copy(pb.at[at:at + TILES, h], full.at[x, :, h], sr_sem).start()
 
-    arrived(view(h, x), t2r_sem)
+    owned = view(h, x)
+    arrived(owned, t2r_sem)
     outs = []
-    for slot in range(2):
-        owned = slot_view(slot, h, x)
-        for n in (2, 1, 3):
-            to = 2 * ((x + n) % XS) + h
-            outs.append(send(owned, owned, os_sem.at[7 * slot + n], or_sem.at[7 * slot + n], to, shard))
-        outs.append(send(owned, owned, os_sem.at[7 * slot], or_sem.at[7 * slot], partner, shard))
+    for n in (2, 1, 3):
+        outs.append(send(owned, owned, os_sem.at[n], or_sem.at[n], 2 * ((x + n) % XS) + h, shard))
+    outs.append(send(owned, owned, os_sem.at[0], or_sem.at[0], partner, shard))
     for copy in outs:
         copy.start()
 
@@ -439,16 +444,15 @@
         for copy in row_sends:
             copy.start()
 
-    def to_partner(slot):
-        for n in (1, 3, 2):
-            piece = slot_view(slot, h, (x + XS - n) % XS)
-            arrived(piece, or_sem.at[7 * slot + n])
-            sem = 7 * slot + 3 + n
-            copy = send(piece, piece, os_sem.at[sem], or_sem.at[sem], partner, shard)
-            copy.start()
-            outs.append(copy)
-
-    to_partner(0)
+    def to_partner(n):
+        piece = view(h, (x + XS - n) % XS)
+        arrived(piece, or_sem.at[n])
+        copy = send(piece, piece, os_sem.at[3 + n], or_sem.at[3 + n], partner, shard)
+        copy.start()
+        outs.append(copy)
+
+    for n in (1, 3, 2):
+        to_partner(n)
 
     def onward(c):
         return send(
@@ -462,13 +466,10 @@
             arrived(full.at[c, :, h], dr_sem.at[c])
             onward(c).start()
 
-    to_partner(1)
     for copy in whole:
         copy.wait()
 
     def factors(n):
-        for index, m in ((0, 0), (4, 1), (6, 3), (5, 2)):
-            arrived(slot_view(n, 1 - h, (x + XS - m) % XS), or_sem.at[7 * n + index])
         on = look[2, 2 * shard + n] > 0
         g = g_own[:, n].reshape(BLK, BLK)
         g = jnp.where(on, g, jnp.zeros_like(g))
@@ -477,6 +478,8 @@
             new = prev[n].reshape(BLK, BLK) + mm(a, b)
             out[n] = jnp.where(on, new, jnp.zeros_like(new))
 
+    for index, m in ((0, 0), (4, 1), (6, 3), (5, 2)):
+        arrived(view(1 - h, (x + XS - m) % XS), or_sem.at[index])
     for n in range(2):
         factors(n)
     for c in range(COLB):
@@ -498,7 +501,7 @@
     swap.wait_send()
     for count, kept in ((16, 0), (16, 1), (32, 1)):
 
-        @pl.when((old_tiles == count) & (old_here.astype(jnp.int32) == kept))
+        @pl.when((jnp.where(summing, HALF, SHARDS) == count) & (old_here.astype(jnp.int32) == kept))
         def _():
             arrived(pvb.at[0:count - kept], p1_sem)
 
@@ -600,7 +603,7 @@
             pltpu.VMEM((8, LANE), jnp.int32),
             pltpu.SMEM((8, LANE), jnp.int32),
             DMA, DMA, DMA((2,)), DMA((3,)), DMA((3,)),
-            DMA, DMA, DMA, DMA, DMA((2,)), DMA, DMA((2,)), DMA, DMA, DMA, DMA, DMA((14,)), DMA((14,)),
+            DMA, DMA, DMA, DMA, DMA((2,)), DMA, DMA((2,)), DMA, DMA, DMA, DMA, DMA((7,)), DMA((7,)),
             DMA((6,)), DMA((3,)), DMA, DMA((7,)), DMA((6,)), DMA, DMA((2,)), DMA((3,)), DMA((3,)), pltpu.SemaphoreType.REGULAR, pltpu.SemaphoreType.REGULAR,
         ],
         compiler_params=pltpu.CompilerParams(

time: 49.1 us -> 48.1 us (0.980)
  Pallas kernels: 48.3 us -> 47.2 us
    pallas_call x1, Pallas kernels: 46.1 us -> 45 us  [body(): pl.pallas_call(step_kernel, out_shape=(pltpu.VMEM((TILES, 2, SUB, COLB *...]
where the time goes in v8:
time: 48.1 us; the launch traced here: 47.9 us
  Pallas kernels  47.2 us (98%)
  between operations  0.64 us (1%)
    pallas_call x1, Pallas kernels, body(): pl.pallas_call(step_kernel, out_shape=(pltpu.VMEM((TILES, 2, SUB, COLB *...  45 us
    pallas_call x1, Pallas kernels, body(): pl.pallas_call(store_kernel, out_shape=(jax.ShapeDtypeStruct((TILES, 2, S...  2.21 us

profile of v8, /device:TPU:1, one launch (start us, length us, event | category | flops | bytes accessed | tf_op | source)
XLA Modules:
  0.0 47.9 jit_solution(497422711153429695)
XLA Ops:
  0.6 45.0 %shampoo_step.1 = (bf16[5,2,16,1536]{3,2,1,0:T(8,128)(2,1)S(1)}, f32[2,512,512]{2,1,0:T(8,128)S(1)}, f32[2,512,512]{2,1,0:T(8,128)S(1)}) custom-call(s32[30]{0:T(128)} %block_owner.1, s32[30]{0:T(128)} %block_row.1, s32[30]{0:T(128)} %block_col.1, bf16[5,2,16,1536]{3,2,1,0:T(8,128)(2,1)} %bitcast.6, f32[2,32,16,512]{3,2,1,0:T(8,128)} %bitcast.4, ...), custom_call_target="tpu_custom_call" | custom-call | tf_op jit(solution)/shard_map/shampoo_step/pallas_call | solution.py:570
  45.7 2.2 %store_results.1 = (bf16[5,2,16,1536]{3,2,1,0:T(8,128)(2,1)}, f32[2,512,512]{2,1,0:T(8,128)}, f32[2,512,512]{2,1,0:T(8,128)}) custom-call(bf16[5,2,16,1536]{3,2,1,0:T(8,128)(2,1)S(1)} %get-tuple-element.9.d_in, f32[2,512,512]{2,1,0:T(8,128)S(1)} %get-tuple-element.10.left_in, f32[2,512,512]{2,1,0:T(8,128)S(1)} %get-tuple-element.11.right_in), custom_call_target="tpu_custom_call" | custom-call | bytes 9437184 | tf_op jit(solution)/shard_map/store_results/pallas_call | solution.py:624

commit v9 on v8

--- a/solution.py
+++ b/solution.py
@@ -183,6 +183,9 @@
         )
 
     loop(3, row_in)
+    fill_tables(tab, block_owner, block_row, block_col)
+    tables = pltpu.make_async_copy(tab, look, tab_sem)
+    tables.start()
     pl.semaphore_wait(rows_in, 3)
     for n in range(1, XS):
         pl.semaphore_signal(
@@ -211,9 +214,6 @@
     def _():
         pltpu.make_async_copy(pvb.at[old_tile], mine, p1r_sem).start()
 
-    fill_tables(tab, block_owner, block_row, block_col)
-    tables = pltpu.make_async_copy(tab, look, tab_sem)
-    tables.start()
     for copy in whole:
         copy.start()
     load.wait()

time: 48.1 us -> 48.9 us (1.017)
  Pallas kernels: 47.2 us -> 48.1 us
    pallas_call x1, Pallas kernels: 45 us -> 45.9 us  [body(): pl.pallas_call(step_kernel, out_shape=(pltpu.VMEM((TILES, 2, SUB, COLB *...]
where the time goes in v9:
time: 48.9 us; the launch traced here: 48.7 us
  Pallas kernels  48.1 us (98%)
  between operations  0.64 us (1%)
    pallas_call x1, Pallas kernels, body(): pl.pallas_call(step_kernel, out_shape=(pltpu.VMEM((TILES, 2, SUB, COLB *...  45.9 us
    pallas_call x1, Pallas kernels, body(): pl.pallas_call(store_kernel, out_shape=(jax.ShapeDtypeStruct((TILES, 2, S...  2.21 us

profile of v9, /device:TPU:1, one launch (start us, length us, event | category | flops | bytes accessed | tf_op | source)
XLA Modules:
  0.0 48.7 jit_solution(14850754846320643486)
XLA Ops:
  0.6 45.9 %shampoo_step.1 = (bf16[5,2,16,1536]{3,2,1,0:T(8,128)(2,1)S(1)}, f32[2,512,512]{2,1,0:T(8,128)S(1)}, f32[2,512,512]{2,1,0:T(8,128)S(1)}) custom-call(s32[30]{0:T(128)} %block_owner.1, s32[30]{0:T(128)} %block_row.1, s32[30]{0:T(128)} %block_col.1, bf16[5,2,16,1536]{3,2,1,0:T(8,128)(2,1)} %bitcast.6, f32[2,32,16,512]{3,2,1,0:T(8,128)} %bitcast.4, ...), custom_call_target="tpu_custom_call" | custom-call | tf_op jit(solution)/shard_map/shampoo_step/pallas_call | solution.py:570
  46.5 2.2 %store_results.1 = (bf16[5,2,16,1536]{3,2,1,0:T(8,128)(2,1)}, f32[2,512,512]{2,1,0:T(8,128)}, f32[2,512,512]{2,1,0:T(8,128)}) custom-call(bf16[5,2,16,1536]{3,2,1,0:T(8,128)(2,1)S(1)} %get-tuple-element.9.d_in, f32[2,512,512]{2,1,0:T(8,128)S(1)} %get-tuple-element.10.left_in, f32[2,512,512]{2,1,0:T(8,128)S(1)} %get-tuple-element.11.right_in), custom_call_target="tpu_custom_call" | custom-call | bytes 9437184 | tf_op jit(solution)/shard_map/store_results/pallas_call | solution.py:624
